TPU v7x, 256 devices: a whole 4x4x8 slice. The times are simulated.
256 devices in a mesh: vocab: 64 (over x, y_hi, z), tensor: 4 (over y_lo, core).
Axes of the slice: x: 4, y: 4 (y_hi: 2, y_lo: 2; y = y_hi * 2 + y_lo), z: 8, core: 2. Of those that a mesh axis runs over, the one named last changes fastest.
Arguments:
- teacher_rows: bfloat16 [512, 3584], P('vocab', 'tensor'), may hold values from -200 to 200
- student_rows: bfloat16 [512, 2304], P('vocab', 'tensor'), may hold values from -200 to 200
- teacher_head: bfloat16 [3584, 131072], P(None, ('vocab', 'tensor')), may hold values from -0.5 to 0.5
- student_head: bfloat16 [2304, 131072], P(None, ('vocab', 'tensor')), may hold values from -0.5 to 0.5
Outputs:
- token_kl: float32 [512], replicated
- student_rows_grad: bfloat16 [512, 2304], P('vocab', 'tensor')
- student_head_grad: bfloat16 [2304, 131072], P(None, ('vocab', 'tensor'))
All inputs are finite; a program needn't handle non-finite values.
Results may differ from a plain program's by a relative error of at most 0.019.
Values may be sent and summed in bfloat16 or wider, within the bound.
No kernel may reach another device: no remote copies, remote signals or barrier semaphores. Data moves between devices by JAX's collectives and lax.ppermute only.
A program may use at most 64 MiB of HBM per device.

v0:
```python
import jax
import jax.numpy as jnp
from jax import lax
from jax.sharding import PartitionSpec as P


def shards(teacher_rows, student_rows, teacher_head, student_head):
    teach_wide, stud_wide = (
        lax.all_gather(teacher_rows, "tensor", axis=1, tiled=True),
        lax.all_gather(student_rows, "tensor", axis=1, tiled=True),
    )
    teach_logits = jnp.dot(
        lax.all_gather(teach_wide, "vocab", axis=0, tiled=True),
        teacher_head,
        preferred_element_type=jnp.float32,
    )
    stud_full = lax.all_gather(stud_wide, "vocab", axis=0, tiled=True)
    stud_logits = jnp.dot(stud_full, student_head, preferred_element_type=jnp.float32)
    teach_peak, stud_peak = lax.pmax(
        (jnp.max(teach_logits, axis=1), jnp.max(stud_logits, axis=1)), ("vocab", "tensor")
    )
    teach_exp = jnp.exp(teach_logits - teach_peak[:, None])
    stud_exp = jnp.exp(stud_logits - stud_peak[:, None])
    teach_total, stud_total, cross = lax.psum(
        (
            jnp.sum(teach_exp, axis=1),
            jnp.sum(stud_exp, axis=1),
            jnp.sum(teach_exp * (teach_logits - stud_logits), axis=1),
        ),
        ("vocab", "tensor"),
    )
    token_kl = (
        cross / teach_total - teach_peak - jnp.log(teach_total) + stud_peak + jnp.log(stud_total)
    )
    logit_grad = (stud_exp / stud_total[:, None] - teach_exp / teach_total[:, None]).astype(
        jnp.bfloat16
    )
    token_grad = lax.psum_scatter(
        lax.dot_general(
            logit_grad, student_head, (((1,), (1,)), ((), ())), preferred_element_type=jnp.float32
        ),
        "vocab",
        scatter_dimension=0,
        tiled=True,
    )
    rows_grad = lax.psum_scatter(
        token_grad.astype(jnp.bfloat16), "tensor", scatter_dimension=1, tiled=True
    )
    head_grad = lax.dot_general(
        stud_full, logit_grad, (((0,), (0,)), ((), ())), preferred_element_type=jnp.float32
    )
    return (token_kl, rows_grad, head_grad.astype(jnp.bfloat16))


def solution(mesh):
    placed = (
        P("vocab", "tensor"),
        P("vocab", "tensor"),
        P(None, ("vocab", "tensor")),
        P(None, ("vocab", "tensor")),
    )
    return jax.shard_map(
        shards,
        mesh=mesh,
        in_specs=placed,
        out_specs=(P(), P("vocab", "tensor"), P(None, ("vocab", "tensor"))),
        check_vma=False,
    )
```

profile of v0, /device:TPU:8, one launch (start us, length us, event | category | flops | bytes accessed | tf_op | source)
XLA Modules:
  0.0 1233.7 jit_solution(4823331702189845684)
XLA Ops:
  7.2 0.0 copy-start
  7.2 0.0 all-gather.6.cloned.1.call-start
  7.2 5.8 all-gather
  13.0 0.7 reshape.11
  13.7 0.0 all-gather.6.cloned.1.call-update
  13.8 0.0 all-gather.4.cloned.1.call-start
  13.8 7.1 all_gather.12
  21.0 0.0 all-gather.4.cloned.1.call-update
  21.0 0.0 reduce-scatter.5.cloned.1.call-start
  21.0 113.9 %all-gather.6.cloned.1.call-done = bf16[512,2304]{1,0:T(8,128)(2,1)} async-done(((bf16[8,2304]{1,0:T(8,128)(2,1)}), bf16[512,2304]{1,0:T(8,128)(2,1)}) %all-gather.6.cloned.1.call-update) | async-done | bytes 2359312 | tf_op jit(solution)/shard_map/all_gather | solution.py:17
  135.0 0.0 copy-done
  135.0 3.1 fusion.4
  138.1 122.2 %all-gather.4.cloned.1.call-done = bf16[512,3584]{1,0:T(8,128)(2,1)} async-done(((bf16[8,3584]{1,0:T(8,128)(2,1)}), bf16[512,3584]{1,0:T(8,128)(2,1)}) %all-gather.4.cloned.1.call-update) | async-done | bytes 3670032 | tf_op jit(solution)/shard_map/all_gather | solution.py:13
  260.3 6.2 fusion.3
  266.5 73.3 %all-reduce.1 = (f32[512]{0:T(512)S(1)}, f32[512]{0:T(512)S(1)}) all-reduce(f32[512]{0:T(512)S(1)} %get-tuple-element.20, f32[512]{0:T(512)S(1)} %get-tuple-element.22), channel_id=1, replica_groups=mesh['vocab'=64,'tensor'=4] {'vocab','tensor'}, use_global_device_ids=true, to_apply=%region_1.0 | all-reduce | flops 1024 | bytes 8192 | tf_op jit(solution)/shard_map/pmax | solution.py:19
  339.8 1.6 multiply_reduce_fusion
  341.4 73.7 %all-reduce = (f32[512]{0:T(512)S(1)}, f32[512]{0:T(512)S(1)}, f32[512]{0:T(512)S(1)}) all-reduce(f32[512]{0:T(512)S(1)} %get-tuple-element.14, f32[512]{0:T(512)S(1)} %get-tuple-element.13, f32[512]{0:T(512)S(1)} %get-tuple-element.12), channel_id=1, replica_groups=mesh['vocab'=64,'tensor'=4] {'vocab','tensor'}, use_global_device_ids=true, to_apply=%region_9.0 | all-reduce | flops 1536 | bytes 12288 | tf_op jit(solution)/shard_map/psum | solution.py:24
  415.1 1.6 subtract_convert_fusion
  416.7 0.0 copy-start.1
  416.7 0.8 copy-done.1
  417.5 3.6 fusion.5
  421.0 0.0 copy-start.2
  421.0 0.0 reduce-scatter.5.cloned.1.call-update
  421.1 0.0 reduce-scatter.7.cloned.1.call-start
  421.1 1.0 copy-done.2
  422.1 4.5 fusion
  426.6 778.5 %reduce-scatter.5.cloned.1.call-done = f32[8,2304]{1,0:T(8,128)} async-done(((f32[512,2304]{1,0:T(8,128)}), f32[8,2304]{1,0:T(8,128)}) %reduce-scatter.5.cloned.1.call-update) | async-done | bytes 73744 | tf_op jit(solution)/shard_map/reduce_scatter | solution.py:38
  1205.1 0.9 convert_element_type.13
  1206.0 1.1 copy.12
  1207.0 0.0 reduce-scatter.7.cloned.1.call-update
  1207.0 0.6 log_add_fusion
  1207.6 4.3 copy.11
  1211.9 13.7 %reduce-scatter.7.cloned.1.call-done = bf16[576,8]{1,0:T(8,128)(2,1)} async-done(((bf16[2304,8]{1,0:T(8,128)(2,1)}), bf16[576,8]{1,0:T(8,128)(2,1)}) %reduce-scatter.7.cloned.1.call-update) | async-done | bytes 9232
  1225.6 1.6 copy.13
  (1 shorter events, 0.0 us)
Async XLA Ops:
  7.2 127.8 %copy-start = (bf16[2304,512]{1,0:T(8,128)(2,1)S(1)}, bf16[2304,512]{1,0:T(8,128)(2,1)}, u32[]{:S(2)}) copy-start(bf16[2304,512]{1,0:T(8,128)(2,1)} %param.7) | copy-start | bytes 7077892
  7.2 127.8 %all-gather.6.cloned.1.call-start = ((), (), s32[]{:S(2)}) async-start(), calls=%async_computation.3 | async-start | bytes 2396160 | tf_op jit(solution)/shard_map/all_gather | solution.py:17
  13.8 246.5 %all-gather.4.cloned.1.call-start = ((), (), s32[]{:S(2)}) async-start(), calls=%async_computation.2 | async-start | bytes 3727360 | tf_op jit(solution)/shard_map/all_gather | solution.py:13
  21.0 1184.1 %reduce-scatter.5.cloned.1.call-start = ((), (), s32[]{:S(2)}) async-start(), calls=%async_computation.4 | async-start | bytes 4792320 | tf_op jit(solution)/shard_map/reduce_scatter | solution.py:38
  416.7 0.8 copy-start.1
  421.0 1.0 copy-start.2
  421.1 804.5 %reduce-scatter.7.cloned.1.call-start = ((), (), s32[]{:S(2)}) async-start(), calls=%async_computation.5 | async-start | bytes 737280
Sparse Core Ops, SparseCore 0:
  13.9 121.0 all-gather.5
  138.6 121.6 all-gather.3
  421.2 783.8 reduce-scatter.4
  1207.5 18.0 reduce-scatter.6
where the time goes:
time: 1240 us; the launch traced here: 1230 us
  waiting for transfers between devices  1030 us (83%)
  blocking collectives  160 us (13%)
  matrix products  17.4 us (1%)
  between operations  13.8 us (1%)
    reduce_scatter x1, waiting for transfers between devices, shards(): lax.psum_scatter(lax.dot_general(logit_grad, student_head, (((1,), (1,)),...  778 us
    all_gather x1, waiting for transfers between devices, shards(): lax.all_gather(teach_wide, 'vocab', axis=0, tiled=True)  122 us
    all_gather x1, waiting for transfers between devices, shards(): stud_full = lax.all_gather(stud_wide, 'vocab', axis=0, tiled=True)  114 us
    psum x1, blocking collectives, shards(): lax.psum((jnp.sum(teach_exp, axis=1), jnp.sum(stud_exp, axis=1), jnp.sum(...  73.7 us
    pmax x1, blocking collectives, shards(): lax.pmax((jnp.max(teach_logits, axis=1), jnp.max(stud_logits, axis=1)), (...  73.3 us
  transfers between devices with their start and end apart: 4, of which 4 were waited for; matrix products, arithmetic and copies ran while one was open for 1% of the time, Pallas kernels for 0%

commit v1 on v0

v1 whole, which is shorter than its diff:
```python
import functools
import jax
import jax.numpy as jnp
from jax import lax
from jax.experimental import pallas as pl
from jax.experimental.pallas import tpu as pltpu
from jax.sharding import Mesh, PartitionSpec as P

F32 = jnp.float32
BF16 = jnp.bfloat16
Y = ("yh", "yl")
VMEM = pl.BlockSpec(memory_space=pltpu.VMEM)
PARAMS = pltpu.CompilerParams(vmem_limit_bytes=40 * 1024 * 1024)


def rows_of(x, y, rx, ry, nx):
    sx = lax.rem(x - rx + nx, nx)
    sy = lax.rem(y - ry + 4, 4)
    return sx * 2 + sy // 2, lax.rem(sy, 2)


def place(parts, full, tokens, nx, x_outer):
    x, c = lax.axis_index("x"), lax.axis_index("c")
    y = lax.axis_index("yh") * 2 + lax.axis_index("yl")
    outer, inner = (nx, 4) if x_outer else (4, nx)
    for half in range(2):
        core = c if half == 0 else 1 - c
        for o in range(outer):
            for i in range(inner):
                block, low = rows_of(x, y, *((o, i) if x_outer else (i, o)), nx)
                full[low * 2 + core, pl.ds(pl.multiple_of(block * tokens, tokens), tokens), :] = parts[
                    half * outer + o
                ][i]


def dot_blocks(full, head, out):
    width = full.shape[2]
    for t in range(4):
        part = jnp.dot(
            full[t], head[t * width : (t + 1) * width, :], preferred_element_type=F32
        )
        if t == 0:
            out[...] = part
        else:
            out[...] += part


def student_kernel(nx, tokens, *refs):
    parts, (head, logits, full) = refs[: 2 * nx], refs[2 * nx :]
    place(parts, full, tokens, nx, True)
    dot_blocks(full, head, logits)


def teacher_kernel(nx, tokens, peers, *refs):
    parts, (head, slog, et_ref, es_ref, stats, full) = refs[:8], refs[8:]
    place(parts, full, tokens, nx, False)
    dot_blocks(full, head, et_ref)
    tl, sl = et_ref[...], slog[...]
    tm = jnp.max(tl, axis=1, keepdims=True)
    sm = jnp.max(sl, axis=1, keepdims=True)
    et, es = jnp.exp(tl - tm), jnp.exp(sl - sm)
    et_ref[...] = et
    es_ref[...] = es
    cols = (
        tm,
        sm,
        jnp.sum(et, axis=1, keepdims=True),
        jnp.sum(es, axis=1, keepdims=True),
        jnp.sum(et * (tl - sl), axis=1, keepdims=True),
    )
    lane = lax.broadcasted_iota(jnp.int32, (tl.shape[0], 128), 1)
    wide = jnp.zeros((tl.shape[0], 128), F32)
    for k, col in enumerate(cols):
        wide = jnp.where(lane == k, col, wide)
    tall = wide.T[:8]
    for p in range(peers):
        stats[p] = tall


def merge(gathered):
    n = gathered.shape[0]
    part = [gathered[p] for p in range(n)]
    tm, sm = part[0][0:1], part[0][1:2]
    for p in range(1, n):
        tm = jnp.maximum(tm, part[p][0:1])
        sm = jnp.maximum(sm, part[p][1:2])
    tt = st = cr = jnp.zeros_like(tm)
    for p in range(n):
        tscale = jnp.exp(part[p][0:1] - tm)
        tt = tt + part[p][2:3] * tscale
        st = st + part[p][3:4] * jnp.exp(part[p][1:2] - sm)
        cr = cr + part[p][4:5] * tscale
    return tm, sm, tt, st, cr


def merge_kernel(gathered, out):
    rows = merge(gathered)
    value = jnp.concatenate(list(rows) + [jnp.zeros_like(rows[0])] * 3, axis=0)
    for p in range(out.shape[0]):
        out[p] = value


def grad_kernel(gathered, own, et, es, head, kl, grad, mine, theirs):
    tm, sm, tt, st, cr = merge(gathered)
    kl[...] = jnp.broadcast_to(cr / tt - tm - jnp.log(tt) + sm + jnp.log(st), kl.shape)
    mine_stats = own[0]
    tscale = jnp.exp(mine_stats[0:1] - tm) / tt
    sscale = jnp.exp(mine_stats[1:2] - sm) / st
    row = lax.broadcasted_iota(jnp.int32, (128, tm.shape[1]), 0)
    wide = jnp.where(row == 0, tscale, jnp.where(row == 1, sscale, 0.0)).T
    grad[...] = (es[...] * wide[:, 1:2] - et[...] * wide[:, 0:1]).astype(BF16)
    c = lax.axis_index("c")
    width = mine.shape[3]
    for low in range(2):
        for out, core in ((theirs, 1 - c), (mine, c)):
            start = pl.multiple_of((low * 2 + core) * width, width)
            value = lax.dot_general(
                grad[...],
                head[pl.ds(start, width), :],
                (((1,), (1,)), ((), ())),
                preferred_element_type=F32,
            )
            out[:, low] = value.reshape(out.shape[0], out.shape[2], width).astype(out.dtype)


def head_kernel(full, grad, out):
    width = full.shape[2]
    for t in range(4):
        out[t * width : (t + 1) * width, :] = lax.dot_general(
            full[t], grad[...], (((0,), (0,)), ((), ())), preferred_element_type=F32
        ).astype(BF16)


def call(kernel, operands, outs, scratch=(), flops=0):
    nbytes = sum(a.size * a.dtype.itemsize for a in list(operands) + list(outs))
    return pl.pallas_call(
        kernel,
        out_shape=outs,
        in_specs=[VMEM] * len(operands),
        out_specs=[VMEM] * len(outs),
        scratch_shapes=list(scratch),
        compiler_params=PARAMS,
        cost_estimate=pl.CostEstimate(flops=flops, bytes_accessed=nbytes, transcendentals=0),
    )(*operands)


def shift(value, axis, n, k):
    return lax.ppermute(value, axis, [(i, (i + k) % n) for i in range(n)])


def shards(sizes, teacher_rows, student_rows, teacher_head, student_head):
    nx, nz = sizes["x"], sizes["z"]
    peers = nx * 4
    wt, ws = teacher_rows.shape[1], student_rows.shape[1]
    rows = teacher_rows.shape[0]
    tokens, total = nz * rows, nx * 2 * nz * rows
    vocab = teacher_head.shape[1]

    both = jnp.concatenate([teacher_rows, student_rows], axis=1)
    both = lax.all_to_all(
        jnp.broadcast_to(both[None], (nz,) + both.shape), "z", 0, 0, tiled=True
    ).reshape(tokens, wt + ws)
    teach, stud = both[:, :wt], both[:, wt:]

    stud = jnp.stack([stud] + [shift(stud, Y, 4, k) for k in range(1, 4)])
    teach = jnp.stack([teach] + [shift(teach, "x", nx, k) for k in range(1, nx)])
    studs = [stud] + [shift(stud, "x", nx, k) for k in range(1, nx)]
    teaches = [teach] + [shift(teach, Y, 4, k) for k in range(1, 4)]
    studs += [shift(part, "c", 2, 1) for part in studs]
    teaches += [shift(part, "c", 2, 1) for part in teaches]

    sds = jax.ShapeDtypeStruct
    stud_logits, stud_full = call(
        functools.partial(student_kernel, nx, tokens),
        studs + [student_head],
        [sds((total, vocab), F32), sds((4, total, ws), BF16)],
        flops=8 * total * ws * vocab,
    )
    et, es, stats = call(
        functools.partial(teacher_kernel, nx, tokens, peers),
        teaches + [teacher_head, stud_logits],
        [sds((total, vocab), F32), sds((total, vocab), F32), sds((peers, 8, total), F32)],
        scratch=[pltpu.VMEM((4, total, wt), BF16)],
        flops=8 * total * wt * vocab,
    )
    gathered = lax.all_to_all(stats, ("x", "yh", "yl"), 0, 0, tiled=True)
    (gathered,) = call(merge_kernel, [gathered], [sds((nz * 2, 8, total), F32)])
    gathered = lax.all_to_all(gathered, ("z", "c"), 0, 0, tiled=True)
    kl, grad, mine, theirs = call(
        grad_kernel,
        [gathered, stats, et, es, student_head],
        [
            sds((8, total), F32),
            sds((total, vocab), BF16),
            sds((nx * 2, 2, tokens, ws), F32),
            sds((nx * 2, 2, tokens, ws), BF16),
        ],
        flops=8 * total * ws * vocab,
    )
    (head_grad,) = call(
        head_kernel,
        [stud_full, grad],
        [sds(student_head.shape, BF16)],
        flops=8 * total * ws * vocab,
    )
    part = (mine + shift(theirs, "c", 2, 1).astype(F32)).astype(BF16)
    part = lax.all_to_all(
        part.reshape(peers, tokens, ws), ("x", "yh", "yl"), 0, 0, tiled=True
    )
    part = jnp.sum(part.astype(F32), axis=0).astype(BF16)
    part = lax.all_to_all(part.reshape(nz, rows, ws), "z", 0, 0, tiled=True)
    rows_grad = jnp.sum(part.astype(F32), axis=0).astype(BF16)
    return kl[0], rows_grad, head_grad


def program(mesh):
    vocab, tensor = ("x", "yh", "z"), ("yl", "c")
    placed = (
        P(vocab, tensor),
        P(vocab, tensor),
        P(None, vocab + tensor),
        P(None, vocab + tensor),
    )
    return jax.shard_map(
        functools.partial(shards, dict(mesh.shape)),
        mesh=mesh,
        in_specs=placed,
        out_specs=(P(), P(vocab, tensor), P(None, vocab + tensor)),
        check_vma=False,
    )


def solution(mesh):
    nz = mesh.shape["vocab"] // 8
    return program(
        Mesh(mesh.devices.reshape(4, 2, nz, 2, 2), ("x", "yh", "z", "yl", "c"))
    )
```

time: 1240 us -> 154 us (0.12)
  waiting for transfers between devices: 1030 us -> 44 us
  blocking collectives: 160 us -> 69.5 us
  starting transfers between devices: 0.16 us -> 24.8 us
  matrix products: 17.4 us -> 0 us
  between operations: 13.8 us -> 0.77 us
    reduce_scatter x1 -> x0, waiting for transfers between devices: 778 us -> none  [shards(): lax.psum_scatter(lax.dot_general(logit_grad, student_head, (((1,), (1,)),...]
    all_gather x2 -> x0, waiting for transfers between devices: 236 us -> none  [the longest x1 122 us: shards(): lax.all_gather(teach_wide, 'vocab', axis=0, tiled=True)]
    psum x1 -> x0, blocking collectives: 73.7 us -> none  [shards(): lax.psum((jnp.sum(teach_exp, axis=1), jnp.sum(stud_exp, axis=1), jnp.sum(...]
    pmax x1 -> x0, blocking collectives: 73.3 us -> none  [shards(): lax.pmax((jnp.max(teach_logits, axis=1), jnp.max(stud_logits, axis=1)), (...]
    all_to_all x0 -> x4, blocking collectives: none -> 69.5 us  [the longest x1 23.8 us: shards(): lax.all_to_all(part.reshape(peers, tokens, ws), ('x', 'yh', 'yl'), 0, 0,...]
    ppermute x0 -> x21, waiting for transfers between devices: none -> 38.9 us  [shift(): return lax.ppermute(value, axis, [(i, (i + k) % n) for i in range(n)])]
    ppermute x0 -> x21, starting transfers between devices: none -> 21.5 us  [shift(): return lax.ppermute(value, axis, [(i, (i + k) % n) for i in range(n)])]
    dot_general x4 -> x0, matrix products: 17.4 us -> none  [the longest x1 6.23 us: shards(): jnp.dot(lax.all_gather(teach_wide, 'vocab', axis=0, tiled=True), teacher_...]
  transfers between devices with their start and end apart: 4 -> 22, of which waited for: 4 -> 10; matrix products, arithmetic and copies ran while one was open for 1% -> 0% of each run, Pallas kernels for 0% -> 3%
where the time goes in v1:
time: 154 us
  blocking collectives  69.5 us (45%)
  waiting for transfers between devices  44 us (29%)
  starting transfers between devices  24.8 us (16%)
  Pallas kernels  10.1 us (7%)
  other arithmetic  4.12 us (3%)
    ppermute x21, waiting for transfers between devices, shift(): return lax.ppermute(value, axis, [(i, (i + k) % n) for i in range(n)])  38.9 us
    all_to_all x1, blocking collectives, shards(): lax.all_to_all(part.reshape(peers, tokens, ws), ('x', 'yh', 'yl'), 0, 0,...  23.8 us
    ppermute x21, starting transfers between devices, shift(): return lax.ppermute(value, axis, [(i, (i + k) % n) for i in range(n)])  21.5 us
    all_to_all x1, blocking collectives, shards(): lax.all_to_all(jnp.broadcast_to(both[None], (nz,) + both.shape), 'z', 0,...  18.7 us
    all_to_all x1, blocking collectives, shards(): gathered = lax.all_to_all(gathered, ('z', 'c'), 0, 0, tiled=True)  15 us
    all_to_all x1, blocking collectives, shards(): gathered = lax.all_to_all(stats, ('x', 'yh', 'yl'), 0, 0, tiled=True)  12 us
    pallas_call x5, Pallas kernels, call(): pl.pallas_call(kernel, out_shape=outs, in_specs=[VMEM] * len(operands), o...  10.1 us
    all_to_all x1, waiting for transfers between devices, shards(): part = lax.all_to_all(part.reshape(nz, rows, ws), 'z', 0, 0, tiled=True)  5.06 us
  transfers between devices with their start and end apart: 22, of which 10 were waited for; matrix products, arithmetic and copies ran while one was open for 0% of the time, Pallas kernels for 3%

profile of v1, /device:TPU:8, one launch (start us, length us, event | category | flops | bytes accessed | tf_op | source)
XLA Modules:
  0.0 154.0 jit_solution(1892601920450926801)
XLA Ops:
  0.6 0.9 pad_maximum_fusion.2
  1.5 18.7 %all_to_all.25 = bf16[8,8,1472]{2,1,0:T(8,128)(2,1)S(1)} all-to-all(bf16[8,8,1472]{2,1,0:T(8,128)(2,1)S(1)} %broadcast_in_dim.2), channel_id=1, replica_groups=mesh['x'=4,'yh'=2,'z'=8,'yl'=2,'c'=2] {'z'}, dimensions={0} | all-to-all | bytes 376832 | tf_op jit(solution)/shard_map/all_to_all | solution.py:160
  20.3 1.7 %collective-permute-start.10 = (bf16[64,576]{1,0:T(8,128)(2,1)S(1)}, bf16[64,576]{1,0:T(8,128)(2,1)S(1)}, u32[]{:S(2)}, u32[]{:S(2)}) collective-permute-start(bf16[64,576]{1,0:T(8,128)(2,1)S(1)} %get-tuple-element.22), channel_id=1, source_target_pairs={{0,2},{2,32},{32,34},{34,0},{1,3},{3,33},{33,35},{35,1},{4,6},{6,3... | collective-permute-start | bytes 221192 | tf_op jit(solution)/shard_map/ppermute | solution.py:148
  22.0 0.9 collective-permute-start.11
  22.9 2.4 %collective-permute-start.12 = (bf16[64,576]{1,0:T(8,128)(2,1)S(1)}, bf16[64,576]{1,0:T(8,128)(2,1)S(1)}, u32[]{:S(2)}, u32[]{:S(2)}) collective-permute-start(bf16[64,576]{1,0:T(8,128)(2,1)S(1)} %get-tuple-element.22), channel_id=1, source_target_pairs={{0,34},{2,0},{32,2},{34,32},{1,35},{3,1},{33,3},{35,33},{4,38},{6,... | collective-permute-start | bytes 221192 | tf_op jit(solution)/shard_map/ppermute | solution.py:148
  25.3 0.0 collective-permute-done.10
  25.3 2.7 %collective-permute-done.11 = bf16[64,576]{1,0:T(8,128)(2,1)S(1)} collective-permute-done((bf16[64,576]{1,0:T(8,128)(2,1)S(1)}, bf16[64,576]{1,0:T(8,128)(2,1)S(1)}, u32[]{:S(2)}, u32[]{:S(2)}) %collective-permute-start.11) | collective-permute-done | bytes 73760 | tf_op jit(solution)/shard_map/ppermute | solution.py:148
  28.0 0.2 collective-permute-done.12
  28.2 0.1 pad_maximum_fusion.1.refs_0_
  28.3 1.6 %collective-permute-start.13 = (bf16[4,64,576]{2,1,0:T(8,128)(2,1)S(1)}, bf16[4,64,576]{2,1,0:T(8,128)(2,1)S(1)}, u32[]{:S(2)}, u32[]{:S(2)}) collective-permute-start(bf16[4,64,576]{2,1,0:T(8,128)(2,1)S(1)} %pad_maximum_fusion.1.refs_0_), channel_id=1, source_target_pairs={{0,64},{64,128},{128,192},{192,0},{1,65},{65,129},{129,193},{193,1... | collective-permute-start | bytes 884744 | tf_op jit(solution)/shard_map/ppermute | solution.py:148
  29.9 2.7 %collective-permute-start.14 = (bf16[4,64,576]{2,1,0:T(8,128)(2,1)S(1)}, bf16[4,64,576]{2,1,0:T(8,128)(2,1)S(1)}, u32[]{:S(2)}, u32[]{:S(2)}) collective-permute-start(bf16[4,64,576]{2,1,0:T(8,128)(2,1)S(1)} %pad_maximum_fusion.1.refs_0_), channel_id=1, source_target_pairs={{0,128},{64,192},{128,0},{192,64},{1,129},{65,193},{129,1},{193,65... | collective-permute-start | bytes 884744 | tf_op jit(solution)/shard_map/ppermute | solution.py:148
  32.6 0.1 collective-permute-start
  32.7 2.9 %collective-permute-start.1 = (bf16[64,896]{1,0:T(8,128)(2,1)S(1)}, bf16[64,896]{1,0:T(8,128)(2,1)S(1)}, u32[]{:S(2)}, u32[]{:S(2)}) collective-permute-start(bf16[64,896]{1,0:T(8,128)(2,1)S(1)} %get-tuple-element.24), channel_id=1, source_target_pairs={{0,128},{64,192},{128,0},{192,64},{1,129},{65,193},{129,1},{193,65... | collective-permute-start | bytes 344072 | tf_op jit(solution)/shard_map/ppermute | solution.py:148
  35.6 0.5 collective-permute-start.2
  36.1 10.7 %collective-permute-done = bf16[64,896]{1,0:T(8,128)(2,1)S(1)} collective-permute-done((bf16[64,896]{1,0:T(8,128)(2,1)S(1)}, bf16[64,896]{1,0:T(8,128)(2,1)S(1)}, u32[]{:S(2)}, u32[]{:S(2)}) %collective-permute-start) | collective-permute-done | bytes 114720 | tf_op jit(solution)/shard_map/ppermute | solution.py:148
  46.8 1.3 collective-permute-start.15
  48.1 0.7 collective-permute-done.1
  48.8 0.1 pad_maximum_fusion.refs_0_
  48.9 0.0 copy-start.1
  48.9 1.4 collective-permute-start.3
  50.3 2.2 %collective-permute-start.4 = (bf16[4,64,896]{2,1,0:T(8,128)(2,1)S(1)}, bf16[4,64,896]{2,1,0:T(8,128)(2,1)S(1)}, u32[]{:S(2)}, u32[]{:S(2)}) collective-permute-start(bf16[4,64,896]{2,1,0:T(8,128)(2,1)S(1)} %pad_maximum_fusion.refs_0_), channel_id=1, source_target_pairs={{0,32},{2,34},{32,0},{34,2},{1,33},{3,35},{33,1},{35,3},{4,36},{6,... | collective-permute-start | bytes 1376264 | tf_op jit(solution)/shard_map/ppermute | solution.py:148
  52.5 0.0 collective-permute-done.14.refs_2_
  52.5 1.7 %collective-permute-start.5 = (bf16[4,64,896]{2,1,0:T(8,128)(2,1)S(1)}, bf16[4,64,896]{2,1,0:T(8,128)(2,1)S(1)}, u32[]{:S(2)}, u32[]{:S(2)}) collective-permute-start(bf16[4,64,896]{2,1,0:T(8,128)(2,1)S(1)} %pad_maximum_fusion.refs_0_), channel_id=1, source_target_pairs={{0,34},{2,0},{32,2},{34,32},{1,35},{3,1},{33,3},{35,33},{4,38},{6,... | collective-permute-start | bytes 1376264 | tf_op jit(solution)/shard_map/ppermute | solution.py:148
  54.1 0.0 collective-permute-done.15.refs_3_
  54.1 0.5 collective-permute-start.18
  54.6 7.6 %collective-permute-done.3.refs_1_ = bf16[4,64,896]{2,1,0:T(8,128)(2,1)S(1)} collective-permute-done((bf16[4,64,896]{2,1,0:T(8,128)(2,1)S(1)}, bf16[4,64,896]{2,1,0:T(8,128)(2,1)S(1)}, u32[]{:S(2)}, u32[]{:S(2)}) %collective-permute-start.3) | collective-permute-done | bytes 458784 | tf_op jit(solution)/shard_map/ppermute | solution.py:148
  62.3 2.9 %collective-permute-done.4.refs_2_ = bf16[4,64,896]{2,1,0:T(8,128)(2,1)S(1)} collective-permute-done((bf16[4,64,896]{2,1,0:T(8,128)(2,1)S(1)}, bf16[4,64,896]{2,1,0:T(8,128)(2,1)S(1)}, u32[]{:S(2)}, u32[]{:S(2)}) %collective-permute-start.4) | collective-permute-done | bytes 458784 | tf_op jit(solution)/shard_map/ppermute | solution.py:148
  65.2 9.1 %collective-permute-done.5.refs_3_ = bf16[4,64,896]{2,1,0:T(8,128)(2,1)S(1)} collective-permute-done((bf16[4,64,896]{2,1,0:T(8,128)(2,1)S(1)}, bf16[4,64,896]{2,1,0:T(8,128)(2,1)S(1)}, u32[]{:S(2)}, u32[]{:S(2)}) %collective-permute-start.5) | collective-permute-done | bytes 458784 | tf_op jit(solution)/shard_map/ppermute | solution.py:148
  74.3 0.0 collective-permute-start.8
  74.3 0.5 collective-permute-start.9
  74.8 0.1 collective-permute-start.19
  74.9 2.3 %collective-permute-done.19.refs_7_ = bf16[4,64,576]{2,1,0:T(8,128)(2,1)S(1)} collective-permute-done((bf16[4,64,576]{2,1,0:T(8,128)(2,1)S(1)}, bf16[4,64,576]{2,1,0:T(8,128)(2,1)S(1)}, u32[]{:S(2)}, u32[]{:S(2)}) %collective-permute-start.19) | collective-permute-done | bytes 294944 | tf_op jit(solution)/shard_map/ppermute | solution.py:148
  77.2 2.0 %shard_map.67 = (f32[512,512]{1,0:T(8,128)S(1)}, bf16[4,512,576]{2,1,0:T(8,128)(2,1)S(1)}) custom-call(bf16[4,64,576]{2,1,0:T(8,128)(2,1)S(1)} %pad_maximum_fusion.1.refs_0_, bf16[4,64,576]{2,1,0:T(8,128)(2,1)S(1)} %collective-permute-done.13.refs_1_, bf16[4,64,576]{2,1,0:T(8,128)(2,1)S(1)} %collective-permute-done.14.refs_2_, ...), custom_call_target="tpu_custom_call" | custom-call | flops 1207959552 | bytes 8126464 | tf_op jit(solution)/shard_map/pallas_call | solution.py:136
  79.3 3.0 %shard_map.68 = (f32[512,512]{1,0:T(8,128)S(1)}, f32[512,512]{1,0:T(8,128)S(1)}, f32[16,8,512]{2,1,0:T(8,128)S(1)}) custom-call(bf16[4,64,896]{2,1,0:T(8,128)(2,1)S(1)} %pad_maximum_fusion.refs_0_, bf16[4,64,896]{2,1,0:T(8,128)(2,1)S(1)} %collective-permute-done.3.refs_1_, bf16[4,64,896]{2,1,0:T(8,128)(2,1)S(1)} %collective-permute-done.4.refs_2_, ...), custom_call_target="tpu_custom_call" | custom-call | flops 1879048192 | bytes 10747904 | tf_op jit(solution)/shard_map/pallas_call | solution.py:136
  82.3 12.0 %all_to_all.26.gathered = f32[16,8,512]{2,1,0:T(8,128)S(1)} all-to-all(f32[16,8,512]{2,1,0:T(8,128)S(1)} %get-tuple-element.13.own), channel_id=1, replica_groups=mesh['x'=4,'yh'=2,'z'=8,'yl'=2,'c'=2] {'x','yh','yl'}, dimensions={0} | all-to-all | bytes 524288 | tf_op jit(solution)/shard_map/all_to_all | solution.py:186
  94.3 0.1 shard_map.69
  94.4 15.0 %all_to_all.27.gathered = f32[16,8,512]{2,1,0:T(8,128)S(1)} all-to-all(f32[16,8,512]{2,1,0:T(8,128)S(1)} %shard_map.69), channel_id=1, replica_groups=mesh['x'=4,'yh'=2,'z'=8,'yl'=2,'c'=2] {'z','c'}, dimensions={0} | all-to-all | bytes 524288 | tf_op jit(solution)/shard_map/all_to_all | solution.py:188
  109.4 2.2 %shard_map.70 = (f32[8,512]{1,0:T(8,128)S(1)}, bf16[512,512]{1,0:T(8,128)(2,1)S(1)}, f32[8,2,64,576]{3,2,1,0:T(8,128)S(1)}, bf16[8,2,64,576]{3,2,1,0:T(8,128)(2,1)S(1)}) custom-call(f32[16,8,512]{2,1,0:T(8,128)S(1)} %all_to_all.27.gathered, f32[16,8,512]{2,1,0:T(8,128)S(1)} %get-tuple-element.13.own, f32[512,512]{1,0:T(8,128)S(1)} %get-tuple-element.14.et, ...), custom_call_target="tpu_custom_call" | custom-call | flops 1207959552 | bytes 9060352 | tf_op jit(solution)/shard_map/pallas_call | solution.py:136
  111.5 1.0 collective-permute-start.20
  112.6 2.7 %collective-permute-done.20 = bf16[8,2,64,576]{3,2,1,0:T(8,128)(2,1)S(1)} collective-permute-done((bf16[8,2,64,576]{3,2,1,0:T(8,128)(2,1)S(1)}, bf16[8,2,64,576]{3,2,1,0:T(8,128)(2,1)S(1)}, u32[]{:S(2)}, u32[]{:S(2)}) %collective-permute-start.20) | collective-permute-done | bytes 1179680 | tf_op jit(solution)/shard_map/ppermute | solution.py:148
  115.2 0.3 add_convert_fusion
  115.6 23.8 %all_to_all.28 = bf16[16,64,576]{2,1,0:T(8,128)(2,1)} all-to-all(bf16[16,64,576]{2,1,0:T(8,128)(2,1)S(1)} %bitcast.14), channel_id=1, replica_groups=mesh['x'=4,'yh'=2,'z'=8,'yl'=2,'c'=2] {'x','yh','yl'}, dimensions={0} | all-to-all | bytes 2359296 | tf_op jit(solution)/shard_map/all_to_all | solution.py:207
  139.4 2.2 %reduce_sum.24 = bf16[64,576]{1,0:T(8,128)(2,1)} reduce(bf16[16,64,576]{2,1,0:T(8,128)(2,1)} %all_to_all.28, bf16[]{:T(256)} %constant.3.clone.1), dimensions={0}, to_apply=%region_0.0 | reduce | flops 552960 | bytes 1253378 | tf_op jit(solution)/shard_map/reduce_sum | solution.py:210
  141.5 3.4 %all-to-all-start.4 = ((bf16[8,8,576]{2,1,0:T(8,128)(2,1)}), bf16[8,8,576]{2,1,0:T(8,128)(2,1)S(1)}, u32[]{:S(2)}, u32[]{:S(2)}) async-start(bf16[8,8,576]{2,1,0:T(8,128)(2,1)} %bitcast.11), calls=%async_computation.4 | async-start | bytes 163840 | tf_op jit(solution)/shard_map/all_to_all | solution.py:211
  144.9 0.6 slice.11
  145.5 2.8 %shard_map.71 = bf16[2304,512]{1,0:T(8,128)(2,1)} custom-call(bf16[4,512,576]{2,1,0:T(8,128)(2,1)S(1)} %get-tuple-element.19.full, bf16[512,512]{1,0:T(8,128)(2,1)S(1)} %get-tuple-element.20.grad), custom_call_target="tpu_custom_call" | custom-call | flops 1207959552 | bytes 5242880 | tf_op jit(solution)/shard_map/pallas_call | solution.py:136
  148.3 5.1 %all-to-all-done.4 = bf16[8,8,576]{2,1,0:T(8,128)(2,1)S(1)} async-done(((bf16[8,8,576]{2,1,0:T(8,128)(2,1)}), bf16[8,8,576]{2,1,0:T(8,128)(2,1)S(1)}, u32[]{:S(2)}, u32[]{:S(2)}) %all-to-all-start.4) | async-done | bytes 73760 | tf_op jit(solution)/shard_map/all_to_all | solution.py:211
  153.4 0.6 reduce_sum.25
  (19 shorter events, 0.1 us)
Async XLA Ops:
  0.6 76.6 %copy-start = (bf16[2304,512]{1,0:T(8,128)(2,1)S(1)}, bf16[2304,512]{1,0:T(8,128)(2,1)}, u32[]{:S(2)}) copy-start(bf16[2304,512]{1,0:T(8,128)(2,1)} %head.1) | copy-start | bytes 7077892
  20.3 5.0 %collective-permute-start.10 = (bf16[64,576]{1,0:T(8,128)(2,1)S(1)}, bf16[64,576]{1,0:T(8,128)(2,1)S(1)}, u32[]{:S(2)}, u32[]{:S(2)}) collective-permute-start(bf16[64,576]{1,0:T(8,128)(2,1)S(1)} %get-tuple-element.22), channel_id=1, source_target_pairs={{0,2},{2,32},{32,34},{34,0},{1,3},{3,33},{33,35},{35,1},{4,6},{6,3... | collective-permute-start | bytes 221192 | tf_op jit(solution)/shard_map/ppermute | solution.py:148
  22.0 6.1 %collective-permute-start.11 = (bf16[64,576]{1,0:T(8,128)(2,1)S(1)}, bf16[64,576]{1,0:T(8,128)(2,1)S(1)}, u32[]{:S(2)}, u32[]{:S(2)}) collective-permute-start(bf16[64,576]{1,0:T(8,128)(2,1)S(1)} %get-tuple-element.22), channel_id=1, source_target_pairs={{0,32},{2,34},{32,0},{34,2},{1,33},{3,35},{33,1},{35,3},{4,36},{6,... | collective-permute-start | bytes 221192 | tf_op jit(solution)/shard_map/ppermute | solution.py:148
  22.9 5.3 %collective-permute-start.12 = (bf16[64,576]{1,0:T(8,128)(2,1)S(1)}, bf16[64,576]{1,0:T(8,128)(2,1)S(1)}, u32[]{:S(2)}, u32[]{:S(2)}) collective-permute-start(bf16[64,576]{1,0:T(8,128)(2,1)S(1)} %get-tuple-element.22), channel_id=1, source_target_pairs={{0,34},{2,0},{32,2},{34,32},{1,35},{3,1},{33,3},{35,33},{4,38},{6,... | collective-permute-start | bytes 221192 | tf_op jit(solution)/shard_map/ppermute | solution.py:148
  28.3 22.0 %collective-permute-start.13 = (bf16[4,64,576]{2,1,0:T(8,128)(2,1)S(1)}, bf16[4,64,576]{2,1,0:T(8,128)(2,1)S(1)}, u32[]{:S(2)}, u32[]{:S(2)}) collective-permute-start(bf16[4,64,576]{2,1,0:T(8,128)(2,1)S(1)} %pad_maximum_fusion.1.refs_0_), channel_id=1, source_target_pairs={{0,64},{64,128},{128,192},{192,0},{1,65},{65,129},{129,193},{193,1... | collective-permute-start | bytes 884744 | tf_op jit(solution)/shard_map/ppermute | solution.py:148
  29.9 22.6 %collective-permute-start.14 = (bf16[4,64,576]{2,1,0:T(8,128)(2,1)S(1)}, bf16[4,64,576]{2,1,0:T(8,128)(2,1)S(1)}, u32[]{:S(2)}, u32[]{:S(2)}) collective-permute-start(bf16[4,64,576]{2,1,0:T(8,128)(2,1)S(1)} %pad_maximum_fusion.1.refs_0_), channel_id=1, source_target_pairs={{0,128},{64,192},{128,0},{192,64},{1,129},{65,193},{129,1},{193,65... | collective-permute-start | bytes 884744 | tf_op jit(solution)/shard_map/ppermute | solution.py:148
  32.6 14.2 %collective-permute-start = (bf16[64,896]{1,0:T(8,128)(2,1)S(1)}, bf16[64,896]{1,0:T(8,128)(2,1)S(1)}, u32[]{:S(2)}, u32[]{:S(2)}) collective-permute-start(bf16[64,896]{1,0:T(8,128)(2,1)S(1)} %get-tuple-element.24), channel_id=1, source_target_pairs={{0,64},{64,128},{128,192},{192,0},{1,65},{65,129},{129,193},{193,1... | collective-permute-start | bytes 344072 | tf_op jit(solution)/shard_map/ppermute | solution.py:148
  32.7 16.1 %collective-permute-start.1 = (bf16[64,896]{1,0:T(8,128)(2,1)S(1)}, bf16[64,896]{1,0:T(8,128)(2,1)S(1)}, u32[]{:S(2)}, u32[]{:S(2)}) collective-permute-start(bf16[64,896]{1,0:T(8,128)(2,1)S(1)} %get-tuple-element.24), channel_id=1, source_target_pairs={{0,128},{64,192},{128,0},{192,64},{1,129},{65,193},{129,1},{193,65... | collective-permute-start | bytes 344072 | tf_op jit(solution)/shard_map/ppermute | solution.py:148
  35.6 13.2 %collective-permute-start.2 = (bf16[64,896]{1,0:T(8,128)(2,1)S(1)}, bf16[64,896]{1,0:T(8,128)(2,1)S(1)}, u32[]{:S(2)}, u32[]{:S(2)}) collective-permute-start(bf16[64,896]{1,0:T(8,128)(2,1)S(1)} %get-tuple-element.24), channel_id=1, source_target_pairs={{0,192},{64,0},{128,64},{192,128},{1,193},{65,1},{129,65},{193,129... | collective-permute-start | bytes 344072 | tf_op jit(solution)/shard_map/ppermute | solution.py:148
  46.8 7.3 %collective-permute-start.15 = (bf16[4,64,576]{2,1,0:T(8,128)(2,1)S(1)}, bf16[4,64,576]{2,1,0:T(8,128)(2,1)S(1)}, u32[]{:S(2)}, u32[]{:S(2)}) collective-permute-start(bf16[4,64,576]{2,1,0:T(8,128)(2,1)S(1)} %pad_maximum_fusion.1.refs_0_), channel_id=1, source_target_pairs={{0,192},{64,0},{128,64},{192,128},{1,193},{65,1},{129,65},{193,129... | collective-permute-start | bytes 884744 | tf_op jit(solution)/shard_map/ppermute | solution.py:148
  48.8 5.3 %collective-permute-start.16 = (bf16[4,64,576]{2,1,0:T(8,128)(2,1)S(1)}, bf16[4,64,576]{2,1,0:T(8,128)(2,1)S(1)}, u32[]{:S(2)}, u32[]{:S(2)}) collective-permute-start(bf16[4,64,576]{2,1,0:T(8,128)(2,1)S(1)} %pad_maximum_fusion.1.refs_0_), channel_id=1, source_target_pairs={{0,1},{1,0},{2,3},{3,2},{4,5},{5,4},{6,7},{7,6},{8,9},{9,8},{10,11... | collective-permute-start | bytes 884744 | tf_op jit(solution)/shard_map/ppermute | solution.py:148
  48.9 30.4 %copy-start.1 = (bf16[3584,512]{1,0:T(8,128)(2,1)S(1)}, bf16[3584,512]{1,0:T(8,128)(2,1)}, u32[]{:S(2)}) copy-start(bf16[3584,512]{1,0:T(8,128)(2,1)} %refs_8_.3) | copy-start | bytes 11010052
  48.9 13.4 %collective-permute-start.3 = (bf16[4,64,896]{2,1,0:T(8,128)(2,1)S(1)}, bf16[4,64,896]{2,1,0:T(8,128)(2,1)S(1)}, u32[]{:S(2)}, u32[]{:S(2)}) collective-permute-start(bf16[4,64,896]{2,1,0:T(8,128)(2,1)S(1)} %pad_maximum_fusion.refs_0_), channel_id=1, source_target_pairs={{0,2},{2,32},{32,34},{34,0},{1,3},{3,33},{33,35},{35,1},{4,6},{6,3... | collective-permute-start | bytes 1376264 | tf_op jit(solution)/shard_map/ppermute | solution.py:148
  50.3 14.9 %collective-permute-start.4 = (bf16[4,64,896]{2,1,0:T(8,128)(2,1)S(1)}, bf16[4,64,896]{2,1,0:T(8,128)(2,1)S(1)}, u32[]{:S(2)}, u32[]{:S(2)}) collective-permute-start(bf16[4,64,896]{2,1,0:T(8,128)(2,1)S(1)} %pad_maximum_fusion.refs_0_), channel_id=1, source_target_pairs={{0,32},{2,34},{32,0},{34,2},{1,33},{3,35},{33,1},{35,3},{4,36},{6,... | collective-permute-start | bytes 1376264 | tf_op jit(solution)/shard_map/ppermute | solution.py:148
  52.5 21.8 %collective-permute-start.5 = (bf16[4,64,896]{2,1,0:T(8,128)(2,1)S(1)}, bf16[4,64,896]{2,1,0:T(8,128)(2,1)S(1)}, u32[]{:S(2)}, u32[]{:S(2)}) collective-permute-start(bf16[4,64,896]{2,1,0:T(8,128)(2,1)S(1)} %pad_maximum_fusion.refs_0_), channel_id=1, source_target_pairs={{0,34},{2,0},{32,2},{34,32},{1,35},{3,1},{33,3},{35,33},{4,38},{6,... | collective-permute-start | bytes 1376264 | tf_op jit(solution)/shard_map/ppermute | solution.py:148
  54.1 20.2 %collective-permute-start.17 = (bf16[4,64,576]{2,1,0:T(8,128)(2,1)S(1)}, bf16[4,64,576]{2,1,0:T(8,128)(2,1)S(1)}, u32[]{:S(2)}, u32[]{:S(2)}) collective-permute-start(bf16[4,64,576]{2,1,0:T(8,128)(2,1)S(1)} %collective-permute-done.13.refs_1_), channel_id=1, source_target_pairs={{0,1},{1,0},{2,3},{3,2},{4,5},{5,4},{6,7},{7,6},{8,9},{9,8},{10,11... | collective-permute-start | bytes 884744 | tf_op jit(solution)/shard_map/ppermute | solution.py:148
  54.1 20.6 %collective-permute-start.18 = (bf16[4,64,576]{2,1,0:T(8,128)(2,1)S(1)}, bf16[4,64,576]{2,1,0:T(8,128)(2,1)S(1)}, u32[]{:S(2)}, u32[]{:S(2)}) collective-permute-start(bf16[4,64,576]{2,1,0:T(8,128)(2,1)S(1)} %collective-permute-done.14.refs_2_), channel_id=1, source_target_pairs={{0,1},{1,0},{2,3},{3,2},{4,5},{5,4},{6,7},{7,6},{8,9},{9,8},{10,11... | collective-permute-start | bytes 884744 | tf_op jit(solution)/shard_map/ppermute | solution.py:148
  62.3 16.9 %collective-permute-start.6 = (bf16[4,64,896]{2,1,0:T(8,128)(2,1)S(1)}, bf16[4,64,896]{2,1,0:T(8,128)(2,1)S(1)}, u32[]{:S(2)}, u32[]{:S(2)}) collective-permute-start(bf16[4,64,896]{2,1,0:T(8,128)(2,1)S(1)} %pad_maximum_fusion.refs_0_), channel_id=1, source_target_pairs={{0,1},{1,0},{2,3},{3,2},{4,5},{5,4},{6,7},{7,6},{8,9},{9,8},{10,11... | collective-permute-start | bytes 1376264 | tf_op jit(solution)/shard_map/ppermute | solution.py:148
  65.2 14.0 %collective-permute-start.7 = (bf16[4,64,896]{2,1,0:T(8,128)(2,1)S(1)}, bf16[4,64,896]{2,1,0:T(8,128)(2,1)S(1)}, u32[]{:S(2)}, u32[]{:S(2)}) collective-permute-start(bf16[4,64,896]{2,1,0:T(8,128)(2,1)S(1)} %collective-permute-done.3.refs_1_), channel_id=1, source_target_pairs={{0,1},{1,0},{2,3},{3,2},{4,5},{5,4},{6,7},{7,6},{8,9},{9,8},{10,11... | collective-permute-start | bytes 1376264 | tf_op jit(solution)/shard_map/ppermute | solution.py:148
  74.3 5.0 %collective-permute-start.8 = (bf16[4,64,896]{2,1,0:T(8,128)(2,1)S(1)}, bf16[4,64,896]{2,1,0:T(8,128)(2,1)S(1)}, u32[]{:S(2)}, u32[]{:S(2)}) collective-permute-start(bf16[4,64,896]{2,1,0:T(8,128)(2,1)S(1)} %collective-permute-done.4.refs_2_), channel_id=1, source_target_pairs={{0,1},{1,0},{2,3},{3,2},{4,5},{5,4},{6,7},{7,6},{8,9},{9,8},{10,11... | collective-permute-start | bytes 1376264 | tf_op jit(solution)/shard_map/ppermute | solution.py:148
  74.3 5.0 %collective-permute-start.9 = (bf16[4,64,896]{2,1,0:T(8,128)(2,1)S(1)}, bf16[4,64,896]{2,1,0:T(8,128)(2,1)S(1)}, u32[]{:S(2)}, u32[]{:S(2)}) collective-permute-start(bf16[4,64,896]{2,1,0:T(8,128)(2,1)S(1)} %collective-permute-done.5.refs_3_), channel_id=1, source_target_pairs={{0,1},{1,0},{2,3},{3,2},{4,5},{5,4},{6,7},{7,6},{8,9},{9,8},{10,11... | collective-permute-start | bytes 1376264 | tf_op jit(solution)/shard_map/ppermute | solution.py:148
  74.8 2.4 %collective-permute-start.19 = (bf16[4,64,576]{2,1,0:T(8,128)(2,1)S(1)}, bf16[4,64,576]{2,1,0:T(8,128)(2,1)S(1)}, u32[]{:S(2)}, u32[]{:S(2)}) collective-permute-start(bf16[4,64,576]{2,1,0:T(8,128)(2,1)S(1)} %collective-permute-done.15.refs_3_), channel_id=1, source_target_pairs={{0,1},{1,0},{2,3},{3,2},{4,5},{5,4},{6,7},{7,6},{8,9},{9,8},{10,11... | collective-permute-start | bytes 884744 | tf_op jit(solution)/shard_map/ppermute | solution.py:148
  111.5 3.7 %collective-permute-start.20 = (bf16[8,2,64,576]{3,2,1,0:T(8,128)(2,1)S(1)}, bf16[8,2,64,576]{3,2,1,0:T(8,128)(2,1)S(1)}, u32[]{:S(2)}, u32[]{:S(2)}) collective-permute-start(bf16[8,2,64,576]{3,2,1,0:T(8,128)(2,1)S(1)} %get-tuple-element.18), channel_id=1, source_target_pairs={{0,1},{1,0},{2,3},{3,2},{4,5},{5,4},{6,7},{7,6},{8,9},{9,8},{10,11... | collective-permute-start | bytes 3538952 | tf_op jit(solution)/shard_map/ppermute | solution.py:148
  141.5 11.8 %all-to-all-start.4 = ((bf16[8,8,576]{2,1,0:T(8,128)(2,1)}), bf16[8,8,576]{2,1,0:T(8,128)(2,1)S(1)}, u32[]{:S(2)}, u32[]{:S(2)}) async-start(bf16[8,8,576]{2,1,0:T(8,128)(2,1)} %bitcast.11), calls=%async_computation.4 | async-start | bytes 163840 | tf_op jit(solution)/shard_map/all_to_all | solution.py:211

commit v2 on v1

v2 whole, which is shorter than its diff:
```python
import functools
import jax
import jax.numpy as jnp
from jax import lax
from jax.experimental import pallas as pl
from jax.experimental.pallas import tpu as pltpu
from jax.sharding import Mesh, PartitionSpec as P

F32 = jnp.float32
BF16 = jnp.bfloat16
Y = ("yh", "yl")
STEPS = (0, 2, 1, 3)
FLIPS = (0, 1, 3, 2)
VMEM = pl.BlockSpec(memory_space=pltpu.VMEM)
PARAMS = pltpu.CompilerParams(vmem_limit_bytes=20 * 1024 * 1024)


def place_kernel(x_outer, *refs):
    parts, out = refs[:4], refs[4]
    tokens = parts[0].shape[1]
    x = lax.axis_index("x")
    y = lax.axis_index("yh") * 2 + lax.axis_index("yl")
    outer, inner = (x, y) if x_outer else (y, x)
    for part, step in zip(parts, STEPS):
        there = lax.rem(outer - step + 4, 4)
        for at, flip in enumerate(FLIPS):
            here = lax.bitwise_xor(inner, flip)
            sx, sy = (there, here) if x_outer else (here, there)
            block = sx * 2 + lax.div(sy, 2)
            rows = pl.ds(pl.multiple_of(block * tokens, tokens), tokens)
            out[lax.rem(sy, 2), rows, :] = part[at]


def student_kernel(extra, own, sibling, head, logits, full):
    c = lax.axis_index("c")
    width = full.shape[2]
    for low in range(2):
        full[low * 2 + c] = own[low, :, extra : extra + width]
        full[low * 2 + 1 - c] = sibling[low, :, extra : extra + width]
    for t in range(4):
        part = jnp.dot(
            full[t], head[t * width : (t + 1) * width, :], preferred_element_type=F32
        )
        if t == 0:
            logits[...] = part
        else:
            logits[...] += part


def teacher_part(columns, head, core, out, first):
    width = head.shape[0] // 4
    for low in range(2):
        start = pl.multiple_of((low * 2 + core) * width, width)
        value = jnp.dot(columns(low), head[pl.ds(start, width), :], preferred_element_type=F32)
        if first and low == 0:
            out[...] = value
        else:
            out[...] += value


def teacher_own_kernel(own, rest, head, out):
    extra = head.shape[0] // 4 - own.shape[2]

    def columns(low):
        return jnp.concatenate([own[low], rest[low, :, :extra]], axis=1)

    teacher_part(columns, head, lax.axis_index("c"), out, True)


def teacher_kernel(sibling, rest, head, begun, slog, et_ref, es_ref, stats):
    extra = head.shape[0] // 4 - sibling.shape[2]

    def columns(low):
        return jnp.concatenate([sibling[low], rest[low, :, :extra]], axis=1)

    et_ref[...] = begun[...]
    teacher_part(columns, head, 1 - lax.axis_index("c"), et_ref, False)
    tl, sl = et_ref[...], slog[...]
    tm = jnp.max(tl, axis=1, keepdims=True)
    sm = jnp.max(sl, axis=1, keepdims=True)
    et, es = jnp.exp(tl - tm), jnp.exp(sl - sm)
    et_ref[...] = et
    es_ref[...] = es
    cols = (
        tm,
        sm,
        jnp.sum(et, axis=1, keepdims=True),
        jnp.sum(es, axis=1, keepdims=True),
        jnp.sum(et * (tl - sl), axis=1, keepdims=True),
    )
    lane = lax.broadcasted_iota(jnp.int32, (tl.shape[0], 128), 1)
    wide = jnp.zeros((tl.shape[0], 128), F32)
    for k, col in enumerate(cols):
        wide = jnp.where(lane == k, col, wide)
    stats[...] = wide.T[:8]


def merge(gathered):
    n = gathered.shape[0]
    part = [gathered[p] for p in range(n)]
    tm, sm = part[0][0:1], part[0][1:2]
    for p in range(1, n):
        tm = jnp.maximum(tm, part[p][0:1])
        sm = jnp.maximum(sm, part[p][1:2])
    tt = st = cr = jnp.zeros_like(tm)
    for p in range(n):
        tscale = jnp.exp(part[p][0:1] - tm)
        tt = tt + part[p][2:3] * tscale
        st = st + part[p][3:4] * jnp.exp(part[p][1:2] - sm)
        cr = cr + part[p][4:5] * tscale
    return tm, sm, tt, st, cr


def merge_kernel(*refs):
    sources, out = refs[:-1], refs[-1]
    part = jnp.stack([r[...] for r in sources]) if len(sources) > 1 else sources[0]
    rows = merge(part)
    value = jnp.concatenate(list(rows) + [jnp.zeros_like(rows[0])] * 3, axis=0)
    for p in range(out.shape[0]):
        out[p] = value


def grad_kernel(gathered, own, et, es, head, kl, grad, theirs):
    tm, sm, tt, st, cr = merge(gathered)
    kl[...] = (cr / tt - tm - jnp.log(tt) + sm + jnp.log(st)).reshape(kl.shape)
    mine_stats = own[...]
    tscale = jnp.exp(mine_stats[0:1] - tm) / tt
    sscale = jnp.exp(mine_stats[1:2] - sm) / st
    row = lax.broadcasted_iota(jnp.int32, (128, tm.shape[1]), 0)
    wide = jnp.where(row == 0, tscale, jnp.where(row == 1, sscale, 0.0)).T
    grad[...] = (es[...] * wide[:, 1:2] - et[...] * wide[:, 0:1]).astype(BF16)
    rows_part(grad, head, 1 - lax.axis_index("c"), theirs)


def rows_part(grad, head, core, out):
    width = out.shape[3]
    for low in range(2):
        start = pl.multiple_of((low * 2 + core) * width, width)
        value = lax.dot_general(
            grad[...],
            head[pl.ds(start, width), :],
            (((1,), (1,)), ((), ())),
            preferred_element_type=F32,
        )
        out[:, low] = value.reshape(out.shape[0], out.shape[2], width).astype(out.dtype)


def mine_kernel(grad, head, mine):
    rows_part(grad, head, lax.axis_index("c"), mine)


def head_kernel(full, grad, out):
    width = full.shape[2]
    for t in range(4):
        out[t * width : (t + 1) * width, :] = lax.dot_general(
            full[t], grad[...], (((0,), (0,)), ((), ())), preferred_element_type=F32
        ).astype(BF16)


def pack_kernel(mine, theirs, out):
    half, width = out.shape[1], mine.shape[3]
    for block in range(mine.shape[0]):
        for low in range(2):
            value = (mine[block, low] + theirs[block, low].astype(F32)).astype(BF16)
            out[block * 2 + low, :, :width] = value[:half]
            out[block * 2 + low, :, width:] = value[half:]


def unpack_kernel(parts, out):
    half, width = parts.shape[1], out.shape[1]
    value = parts[0].astype(F32)
    for p in range(1, parts.shape[0]):
        value = value + parts[p].astype(F32)
    value = value.astype(BF16)
    out[:half] = value[:, :width]
    out[half:] = value[:, width:]


def call(kernel, operands, outs, scratch=(), flops=0):
    nbytes = sum(a.size * a.dtype.itemsize for a in list(operands) + list(outs))
    return pl.pallas_call(
        kernel,
        out_shape=outs,
        in_specs=[VMEM] * len(operands),
        out_specs=[VMEM] * len(outs),
        scratch_shapes=list(scratch),
        compiler_params=PARAMS,
        cost_estimate=pl.CostEstimate(flops=flops, bytes_accessed=nbytes, transcendentals=0),
    )(*operands)


def shift(value, axis, n, k):
    return lax.ppermute(value, axis, [(i, (i + k) % n) for i in range(n)])


def flip(value, axis, k):
    return lax.ppermute(value, axis, [(i, i ^ k) for i in range(4)])


def shards(sizes, teacher_rows, student_rows, teacher_head, student_head):
    nz = sizes["z"]
    wt, ws = teacher_rows.shape[1], student_rows.shape[1]
    rows = teacher_rows.shape[0]
    tokens, total = nz * rows, 8 * nz * rows
    vocab = teacher_head.shape[1]
    cut = (wt + ws) // 256 * 128 + 128

    fill = -(wt + ws) % 128
    both = jnp.concatenate(
        [teacher_rows, student_rows, jnp.zeros((rows, fill), BF16)], axis=1
    )
    both = lax.all_to_all(
        jnp.broadcast_to(both[None], (nz,) + both.shape), "z", 0, 0, tiled=True
    ).reshape(1, tokens, wt + ws + fill)
    a, b = both[:, :, :cut], both[:, :, cut:]
    for k in (1, 3):
        more = flip(a, "x", k), flip(b, Y, k)
        a, b = jnp.concatenate([a, more[0]]), jnp.concatenate([b, more[1]])
        a, b = lax.optimization_barrier((a, b))
    a_1, a_3 = shift(a, Y, 4, 1), shift(a, Y, 4, 3)
    b_1, b_3, b_2 = (shift(b, "x", 4, k) for k in (1, 3, 2))
    late, b_1, b_3 = lax.optimization_barrier((a, b_1, b_3))
    a_parts, b_parts = [a, shift(late, Y, 4, 2), a_1, a_3], [b, b_2, b_1, b_3]

    sds = jax.ShapeDtypeStruct
    (b_own,) = call(
        functools.partial(place_kernel, True), b_parts, [sds((2, total, wt + ws + fill - cut), BF16)]
    )
    b_sib = shift(b_own, "c", 2, 1)
    (a_own,) = call(functools.partial(place_kernel, False), a_parts, [sds((2, total, cut), BF16)])
    a_sib = shift(a_own, "c", 2, 1)
    stud_logits, stud_full = call(
        functools.partial(student_kernel, wt - cut),
        [b_own, b_sib, student_head],
        [sds((total, vocab), F32), sds((4, total, ws), BF16)],
        flops=8 * total * ws * vocab,
    )
    (teach_part,) = call(
        teacher_own_kernel,
        [a_own, b_own, teacher_head],
        [sds((total, vocab), F32)],
        flops=4 * total * wt * vocab,
    )
    et, es, stats = call(
        teacher_kernel,
        [a_sib, b_sib, teacher_head, teach_part, stud_logits],
        [sds((total, vocab), F32), sds((total, vocab), F32), sds((8, total), F32)],
        flops=4 * total * wt * vocab,
    )
    (gathered,) = call(
        merge_kernel, [stats, shift(stats, "c", 2, 1)], [sds((16, 8, total), F32)]
    )
    gathered = lax.all_to_all(gathered, ("x", "yh", "yl"), 0, 0, tiled=True)
    (gathered,) = call(merge_kernel, [gathered], [sds((nz, 8, total), F32)])
    gathered = lax.all_to_all(gathered, "z", 0, 0, tiled=True)
    kl, grad, theirs = call(
        grad_kernel,
        [gathered, stats, et, es, student_head],
        [sds((total,), F32), sds((total, vocab), BF16), sds((8, 2, tokens, ws), BF16)],
        flops=4 * total * ws * vocab,
    )
    theirs = shift(theirs, "c", 2, 1)
    (mine,) = call(
        mine_kernel,
        [grad, student_head],
        [sds((8, 2, tokens, ws), F32)],
        flops=4 * total * ws * vocab,
    )
    (part,) = call(pack_kernel, [mine, theirs], [sds((16, tokens // 2, 2 * ws), BF16)])
    part = lax.all_to_all(part, ("x", "yh", "yl"), 0, 0, tiled=True)
    (part,) = call(unpack_kernel, [part], [sds((tokens, ws), BF16)])
    part, grad = lax.optimization_barrier((part, grad))
    (head_grad,) = call(
        head_kernel,
        [stud_full, grad],
        [sds(student_head.shape, BF16)],
        flops=8 * total * ws * vocab,
    )
    part = lax.all_to_all(part.reshape(nz, rows, ws), "z", 0, 0, tiled=True)
    rows_grad = jnp.sum(part.astype(F32), axis=0).astype(BF16)
    return kl, rows_grad, head_grad


def program(mesh):
    vocab, tensor = ("x", "yh", "z"), ("yl", "c")
    placed = (
        P(vocab, tensor),
        P(vocab, tensor),
        P(None, vocab + tensor),
        P(None, vocab + tensor),
    )
    return jax.shard_map(
        functools.partial(shards, dict(mesh.shape)),
        mesh=mesh,
        in_specs=placed,
        out_specs=(P(), P(vocab, tensor), P(None, vocab + tensor)),
        check_vma=False,
    )


def solution(mesh):
    nz = mesh.shape["vocab"] // 8
    return program(
        Mesh(mesh.devices.reshape(4, 2, nz, 2, 2), ("x", "yh", "z", "yl", "c"))
    )
```

time: 154 us -> 134 us (0.87)
  waiting for transfers between devices: 44 us -> 32.6 us
  starting transfers between devices: 24.8 us -> 19.6 us
  other arithmetic: 4.12 us -> 0.73 us
  blocking collectives: 69.5 us -> 66.3 us
  Pallas kernels: 10.1 us -> 11.9 us
    ppermute x21 -> x10, waiting for transfers between devices: 38.9 us -> 20.2 us  [shift(): return lax.ppermute(value, axis, [(i, (i + k) % n) for i in range(n)])]
    ppermute x21 -> x10, starting transfers between devices: 21.5 us -> 8.94 us  [shift(): return lax.ppermute(value, axis, [(i, (i + k) % n) for i in range(n)])]
    ppermute x0 -> x4, starting transfers between devices: none -> 7.28 us  [flip(): return lax.ppermute(value, axis, [(i, i ^ k) for i in range(4)])]
    ppermute x0 -> x4, waiting for transfers between devices: none -> 6.71 us  [flip(): return lax.ppermute(value, axis, [(i, i ^ k) for i in range(4)])]
    all_to_all x3, blocking collectives: 50.8 us -> 47.6 us  [the longest x1 22.2 us: shards(): part = lax.all_to_all(part, ('x', 'yh', 'yl'), 0, 0, tiled=True)]
    reduce_sum x1 -> x0, other arithmetic: 2.16 us -> none  [shards(): part = jnp.sum(part.astype(F32), axis=0).astype(BF16)]
    pallas_call x5 -> x12, Pallas kernels: 10.1 us -> 11.9 us  [call(): pl.pallas_call(kernel, out_shape=outs, in_specs=[VMEM] * len(operands), o...]
  transfers between devices with their start and end apart: 22 -> 15, of which waited for: 10 -> 10; matrix products, arithmetic and copies ran while one was open for 0% -> 0% of each run, Pallas kernels for 3% -> 5%
where the time goes in v2:
time: 134 us; the launch traced here: 133 us
  blocking collectives  66.3 us (49%)
  waiting for transfers between devices  32.6 us (24%)
  starting transfers between devices  19.6 us (15%)
  Pallas kernels  11.9 us (9%)
    all_to_all x1, blocking collectives, shards(): part = lax.all_to_all(part, ('x', 'yh', 'yl'), 0, 0, tiled=True)  22.2 us
    ppermute x10, waiting for transfers between devices, shift(): return lax.ppermute(value, axis, [(i, (i + k) % n) for i in range(n)])  20.2 us
    all_to_all x1, blocking collectives, shards(): lax.all_to_all(jnp.broadcast_to(both[None], (nz,) + both.shape), 'z', 0,...  18.7 us
    all_to_all x1, blocking collectives, shards(): gathered = lax.all_to_all(gathered, ('x', 'yh', 'yl'), 0, 0, tiled=True)  13.3 us
    all_to_all x1, blocking collectives, shards(): gathered = lax.all_to_all(gathered, 'z', 0, 0, tiled=True)  12.1 us
    pallas_call x12, Pallas kernels, call(): pl.pallas_call(kernel, out_shape=outs, in_specs=[VMEM] * len(operands), o...  11.9 us
    ppermute x10, starting transfers between devices, shift(): return lax.ppermute(value, axis, [(i, (i + k) % n) for i in range(n)])  8.94 us
    ppermute x4, starting transfers between devices, flip(): return lax.ppermute(value, axis, [(i, i ^ k) for i in range(4)])  7.28 us
  transfers between devices with their start and end apart: 15, of which 10 were waited for; matrix products, arithmetic and copies ran while one was open for 0% of the time, Pallas kernels for 5%

profile of v2, /device:TPU:8, one launch (start us, length us, event | category | flops | bytes accessed | tf_op | source)
XLA Modules:
  0.0 133.0 jit_solution(13064051038140715586)
XLA Ops:
  0.6 0.8 concatenate.15
  1.5 18.7 %all_to_all.25 = bf16[8,8,1536]{2,1,0:T(8,128)(2,1)S(1)} all-to-all(bf16[8,8,1536]{2,1,0:T(8,128)(2,1)S(1)} %broadcast_in_dim.10), channel_id=1, replica_groups=mesh['x'=4,'yh'=2,'z'=8,'yl'=2,'c'=2] {'z'}, dimensions={0} | all-to-all | bytes 393216 | tf_op jit(solution)/shard_map/all_to_all | solution.py:212
  20.2 0.5 collective-permute-start.1
  20.7 1.5 %collective-permute-start = (bf16[1,64,768]{2,1,0:T(8,128)(2,1)S(1)}, bf16[1,64,768]{2,1,0:T(8,128)(2,1)S(1)}, u32[]{:S(2)}, u32[]{:S(2)}) collective-permute-start(bf16[1,64,768]{2,1,0:T(8,128)(2,1)S(1)} %get-tuple-element.38), channel_id=1, source_target_pairs={{0,64},{64,0},{128,192},{192,128},{1,65},{65,1},{129,193},{193,129... | collective-permute-start | bytes 294920 | tf_op jit(solution)/shard_map/ppermute | solution.py:197
  22.2 2.7 %collective-permute-done.1 = bf16[1,64,768]{2,1,0:T(8,128)(2,1)S(1)} collective-permute-done((bf16[1,64,768]{2,1,0:T(8,128)(2,1)S(1)}, bf16[1,64,768]{2,1,0:T(8,128)(2,1)S(1)}, u32[]{:S(2)}, u32[]{:S(2)}) %collective-permute-start.1) | collective-permute-done | bytes 98336 | tf_op jit(solution)/shard_map/ppermute | solution.py:197
  24.9 0.4 collective-permute-done
  25.4 2.8 %collective-permute-start.2 = (bf16[2,64,768]{2,1,0:T(8,128)(2,1)S(1)}, bf16[2,64,768]{2,1,0:T(8,128)(2,1)S(1)}, u32[]{:S(2)}, u32[]{:S(2)}) collective-permute-start(bf16[2,64,768]{2,1,0:T(8,128)(2,1)S(1)} %pad_maximum_fusion.2), channel_id=1, source_target_pairs={{0,192},{64,128},{128,64},{192,0},{1,193},{65,129},{129,65},{193,1... | collective-permute-start | bytes 589832 | tf_op jit(solution)/shard_map/ppermute | solution.py:197
  28.2 2.4 %collective-permute-start.3 = (bf16[2,64,768]{2,1,0:T(8,128)(2,1)S(1)}, bf16[2,64,768]{2,1,0:T(8,128)(2,1)S(1)}, u32[]{:S(2)}, u32[]{:S(2)}) collective-permute-start(bf16[2,64,768]{2,1,0:T(8,128)(2,1)S(1)} %pad_maximum_fusion.3), channel_id=1, source_target_pairs={{0,34},{2,32},{32,2},{34,0},{1,35},{3,33},{33,3},{35,1},{4,38},{6,... | collective-permute-start | bytes 589832 | tf_op jit(solution)/shard_map/ppermute | solution.py:197
  30.6 1.7 %collective-permute-done.2 = bf16[2,64,768]{2,1,0:T(8,128)(2,1)S(1)} collective-permute-done((bf16[2,64,768]{2,1,0:T(8,128)(2,1)S(1)}, bf16[2,64,768]{2,1,0:T(8,128)(2,1)S(1)}, u32[]{:S(2)}, u32[]{:S(2)}) %collective-permute-start.2) | collective-permute-done | bytes 196640 | tf_op jit(solution)/shard_map/ppermute | solution.py:197
  32.4 1.9 %collective-permute-done.3 = bf16[2,64,768]{2,1,0:T(8,128)(2,1)S(1)} collective-permute-done((bf16[2,64,768]{2,1,0:T(8,128)(2,1)S(1)}, bf16[2,64,768]{2,1,0:T(8,128)(2,1)S(1)}, u32[]{:S(2)}, u32[]{:S(2)}) %collective-permute-start.3) | collective-permute-done | bytes 196640 | tf_op jit(solution)/shard_map/ppermute | solution.py:197
  34.3 1.6 %collective-permute-start.5 = (bf16[4,64,768]{2,1,0:T(8,128)(2,1)S(1)}, bf16[4,64,768]{2,1,0:T(8,128)(2,1)S(1)}, u32[]{:S(2)}, u32[]{:S(2)}) collective-permute-start(bf16[4,64,768]{2,1,0:T(8,128)(2,1)S(1)} %pad_maximum_fusion.1.refs_0_), channel_id=1, source_target_pairs={{0,192},{64,0},{128,64},{192,128},{1,193},{65,1},{129,65},{193,129... | collective-permute-start | bytes 1179656 | tf_op jit(solution)/shard_map/ppermute | solution.py:193
  35.9 0.5 collective-permute-start.4
  36.4 1.1 collective-permute-start.10
  37.5 2.1 %collective-permute-start.8 = (bf16[4,64,768]{2,1,0:T(8,128)(2,1)S(1)}, bf16[4,64,768]{2,1,0:T(8,128)(2,1)S(1)}, u32[]{:S(2)}, u32[]{:S(2)}) collective-permute-start(bf16[4,64,768]{2,1,0:T(8,128)(2,1)S(1)} %pad_maximum_fusion.refs_0_), channel_id=1, source_target_pairs={{0,34},{2,0},{32,2},{34,32},{1,35},{3,1},{33,3},{35,33},{4,38},{6,... | collective-permute-start | bytes 1179656 | tf_op jit(solution)/shard_map/ppermute | solution.py:193
  39.6 0.3 collective-permute-start.7
  39.9 5.1 %collective-permute-done.5.refs_3_ = bf16[4,64,768]{2,1,0:T(8,128)(2,1)S(1)} collective-permute-done((bf16[4,64,768]{2,1,0:T(8,128)(2,1)S(1)}, bf16[4,64,768]{2,1,0:T(8,128)(2,1)S(1)}, u32[]{:S(2)}, u32[]{:S(2)}) %collective-permute-start.5) | collective-permute-done | bytes 393248 | tf_op jit(solution)/shard_map/ppermute | solution.py:193
  45.0 6.0 %collective-permute-done.4.refs_2_ = bf16[4,64,768]{2,1,0:T(8,128)(2,1)S(1)} collective-permute-done((bf16[4,64,768]{2,1,0:T(8,128)(2,1)S(1)}, bf16[4,64,768]{2,1,0:T(8,128)(2,1)S(1)}, u32[]{:S(2)}, u32[]{:S(2)}) %collective-permute-start.4) | collective-permute-done | bytes 393248 | tf_op jit(solution)/shard_map/ppermute | solution.py:193
  51.0 2.9 %collective-permute-start.6 = (bf16[4,64,768]{2,1,0:T(8,128)(2,1)S(1)}, bf16[4,64,768]{2,1,0:T(8,128)(2,1)S(1)}, u32[]{:S(2)}, u32[]{:S(2)}) collective-permute-start(bf16[4,64,768]{2,1,0:T(8,128)(2,1)S(1)} %pad_maximum_fusion.refs_0_), channel_id=1, source_target_pairs={{0,32},{2,34},{32,0},{34,2},{1,33},{3,35},{33,1},{35,3},{4,36},{6,... | collective-permute-start | bytes 1179656 | tf_op jit(solution)/shard_map/ppermute | solution.py:193
  53.9 0.0 collective-permute-done.10.refs_1_
  53.9 0.1 shard_map.68.rest.own
  54.0 0.1 collective-permute-start.11
  54.1 0.0 collective-permute-done.8.refs_3_
  54.1 0.0 collective-permute-done.7.refs_2_
  54.2 6.1 %collective-permute-done.6.refs_1_ = bf16[4,64,768]{2,1,0:T(8,128)(2,1)S(1)} collective-permute-done((bf16[4,64,768]{2,1,0:T(8,128)(2,1)S(1)}, bf16[4,64,768]{2,1,0:T(8,128)(2,1)S(1)}, u32[]{:S(2)}, u32[]{:S(2)}) %collective-permute-start.6) | collective-permute-done | bytes 393248 | tf_op jit(solution)/shard_map/ppermute | solution.py:193
  60.3 0.1 shard_map.67.own
  60.4 0.0 copy-start
  60.4 0.1 collective-permute-start.9
  60.5 1.3 shard_map.69.begun
  61.8 0.0 collective-permute-done.11.sibling.rest
  61.8 0.3 copy-done
  62.1 1.8 %shard_map.70 = (f32[512,512]{1,0:T(8,128)S(1)}, bf16[4,512,576]{2,1,0:T(8,128)(2,1)S(1)}) custom-call(bf16[2,512,768]{2,1,0:T(8,128)(2,1)S(1)} %shard_map.68.rest.own, bf16[2,512,768]{2,1,0:T(8,128)(2,1)S(1)} %collective-permute-done.11.sibling.rest, bf16[2304,512]{1,0:T(8,128)(2,1)S(1)} %copy-done), custom_call_target="tpu_custom_call" | custom-call | flops 1207959552 | bytes 8912896 | tf_op jit(solution)/shard_map/pallas_call | solution.py:181
  63.9 0.0 collective-permute-done.9.sibling
  63.9 1.7 %shard_map.71 = (f32[512,512]{1,0:T(8,128)S(1)}, f32[512,512]{1,0:T(8,128)S(1)}, f32[8,512]{1,0:T(8,128)S(1)}) custom-call(bf16[2,512,768]{2,1,0:T(8,128)(2,1)S(1)} %collective-permute-done.9.sibling, bf16[2,512,768]{2,1,0:T(8,128)(2,1)S(1)} %collective-permute-done.11.sibling.rest, bf16[3584,512]{1,0:T(8,128)(2,1)S(1)} %copy-done.1, ...), custom_call_target="tpu_custom_call" | custom-call | flops 939524096 | bytes 11026432 | tf_op jit(solution)/shard_map/pallas_call | solution.py:181
  65.6 0.3 collective-permute-start.12
  65.8 1.0 collective-permute-done.12.refs_1_
  66.9 13.3 %all_to_all.26.refs_0_ = f32[16,8,512]{2,1,0:T(8,128)S(1)} all-to-all(f32[16,8,512]{2,1,0:T(8,128)S(1)} %shard_map.72), channel_id=1, replica_groups=mesh['x'=4,'yh'=2,'z'=8,'yl'=2,'c'=2] {'x','yh','yl'}, dimensions={0} | all-to-all | bytes 524288 | tf_op jit(solution)/shard_map/all_to_all | solution.py:253
  80.2 0.1 shard_map.73
  80.3 12.1 %all_to_all.27.gathered = f32[8,8,512]{2,1,0:T(8,128)S(1)} all-to-all(f32[8,8,512]{2,1,0:T(8,128)S(1)} %shard_map.73), channel_id=1, replica_groups=mesh['x'=4,'yh'=2,'z'=8,'yl'=2,'c'=2] {'z'}, dimensions={0} | all-to-all | bytes 262144 | tf_op jit(solution)/shard_map/all_to_all | solution.py:255
  92.4 1.8 %shard_map.74 = (f32[512]{0:T(512)}, bf16[512,512]{1,0:T(8,128)(2,1)S(1)}, bf16[8,2,64,576]{3,2,1,0:T(8,128)(2,1)S(1)}) custom-call(f32[8,8,512]{2,1,0:T(8,128)S(1)} %all_to_all.27.gathered, f32[8,512]{1,0:T(8,128)S(1)} %get-tuple-element.28.refs_0_.own, f32[512,512]{1,0:T(8,128)S(1)} %get-tuple-element.29.et, f32[512,512]{1,0:T(8,128)S(1)} %get-tuple-element.30.es, ...), custom_call_target="tpu_custom_call" | custom-call | flops 603979776 | bytes 6309888 | tf_op jit(solution)/shard_map/pallas_call | solution.py:181
  94.3 1.0 shard_map.75.mine
  95.3 2.0 %collective-permute-done.13.theirs = bf16[8,2,64,576]{3,2,1,0:T(8,128)(2,1)S(1)} collective-permute-done((bf16[8,2,64,576]{3,2,1,0:T(8,128)(2,1)S(1)}, bf16[8,2,64,576]{3,2,1,0:T(8,128)(2,1)S(1)}, u32[]{:S(2)}, u32[]{:S(2)}) %collective-permute-start.13) | collective-permute-done | bytes 1179680 | tf_op jit(solution)/shard_map/ppermute | solution.py:193
  97.3 0.3 shard_map.76
  97.6 22.2 %all_to_all.28.parts = bf16[16,32,1152]{2,1,0:T(8,128)(2,1)S(1)} all-to-all(bf16[16,32,1152]{2,1,0:T(8,128)(2,1)S(1)} %shard_map.76), channel_id=1, replica_groups=mesh['x'=4,'yh'=2,'z'=8,'yl'=2,'c'=2] {'x','yh','yl'}, dimensions={0} | all-to-all | bytes 2359296 | tf_op jit(solution)/shard_map/all_to_all | solution.py:270
  119.8 0.8 shard_map.77
  120.6 3.4 %all-to-all-start.4 = ((bf16[8,8,576]{2,1,0:T(8,128)(2,1)}), bf16[8,8,576]{2,1,0:T(8,128)(2,1)S(1)}, u32[]{:S(2)}, u32[]{:S(2)}) async-start(bf16[8,8,576]{2,1,0:T(8,128)(2,1)} %bitcast.1), calls=%async_computation.4 | async-start | bytes 163840 | tf_op jit(solution)/shard_map/all_to_all | solution.py:279
  123.9 2.8 %shard_map.78 = bf16[2304,512]{1,0:T(8,128)(2,1)} custom-call(bf16[4,512,576]{2,1,0:T(8,128)(2,1)S(1)} %get-tuple-element.35.full, bf16[512,512]{1,0:T(8,128)(2,1)S(1)} %get-tuple-element.36.grad), custom_call_target="tpu_custom_call" | custom-call | flops 1207959552 | bytes 5242880 | tf_op jit(solution)/shard_map/pallas_call | solution.py:181
  126.8 5.6 %all-to-all-done.4 = bf16[8,8,576]{2,1,0:T(8,128)(2,1)S(1)} async-done(((bf16[8,8,576]{2,1,0:T(8,128)(2,1)}), bf16[8,8,576]{2,1,0:T(8,128)(2,1)S(1)}, u32[]{:S(2)}, u32[]{:S(2)}) %all-to-all-start.4) | async-done | bytes 73760 | tf_op jit(solution)/shard_map/all_to_all | solution.py:279
  132.4 0.6 reduce_sum.12
  (11 shorter events, 0.2 us)
Async XLA Ops:
  20.2 4.7 %collective-permute-start.1 = (bf16[1,64,768]{2,1,0:T(8,128)(2,1)S(1)}, bf16[1,64,768]{2,1,0:T(8,128)(2,1)S(1)}, u32[]{:S(2)}, u32[]{:S(2)}) collective-permute-start(bf16[1,64,768]{2,1,0:T(8,128)(2,1)S(1)} %get-tuple-element.37), channel_id=1, source_target_pairs={{0,2},{2,0},{32,34},{34,32},{1,3},{3,1},{33,35},{35,33},{4,6},{6,4... | collective-permute-start | bytes 294920 | tf_op jit(solution)/shard_map/ppermute | solution.py:197
  20.7 4.6 %collective-permute-start = (bf16[1,64,768]{2,1,0:T(8,128)(2,1)S(1)}, bf16[1,64,768]{2,1,0:T(8,128)(2,1)S(1)}, u32[]{:S(2)}, u32[]{:S(2)}) collective-permute-start(bf16[1,64,768]{2,1,0:T(8,128)(2,1)S(1)} %get-tuple-element.38), channel_id=1, source_target_pairs={{0,64},{64,0},{128,192},{192,128},{1,65},{65,1},{129,193},{193,129... | collective-permute-start | bytes 294920 | tf_op jit(solution)/shard_map/ppermute | solution.py:197
  25.4 7.0 %collective-permute-start.2 = (bf16[2,64,768]{2,1,0:T(8,128)(2,1)S(1)}, bf16[2,64,768]{2,1,0:T(8,128)(2,1)S(1)}, u32[]{:S(2)}, u32[]{:S(2)}) collective-permute-start(bf16[2,64,768]{2,1,0:T(8,128)(2,1)S(1)} %pad_maximum_fusion.2), channel_id=1, source_target_pairs={{0,192},{64,128},{128,64},{192,0},{1,193},{65,129},{129,65},{193,1... | collective-permute-start | bytes 589832 | tf_op jit(solution)/shard_map/ppermute | solution.py:197
  28.2 6.1 %collective-permute-start.3 = (bf16[2,64,768]{2,1,0:T(8,128)(2,1)S(1)}, bf16[2,64,768]{2,1,0:T(8,128)(2,1)S(1)}, u32[]{:S(2)}, u32[]{:S(2)}) collective-permute-start(bf16[2,64,768]{2,1,0:T(8,128)(2,1)S(1)} %pad_maximum_fusion.3), channel_id=1, source_target_pairs={{0,34},{2,32},{32,2},{34,0},{1,35},{3,33},{33,3},{35,1},{4,38},{6,... | collective-permute-start | bytes 589832 | tf_op jit(solution)/shard_map/ppermute | solution.py:197
  34.3 10.7 %collective-permute-start.5 = (bf16[4,64,768]{2,1,0:T(8,128)(2,1)S(1)}, bf16[4,64,768]{2,1,0:T(8,128)(2,1)S(1)}, u32[]{:S(2)}, u32[]{:S(2)}) collective-permute-start(bf16[4,64,768]{2,1,0:T(8,128)(2,1)S(1)} %pad_maximum_fusion.1.refs_0_), channel_id=1, source_target_pairs={{0,192},{64,0},{128,64},{192,128},{1,193},{65,1},{129,65},{193,129... | collective-permute-start | bytes 1179656 | tf_op jit(solution)/shard_map/ppermute | solution.py:193
  35.9 15.0 %collective-permute-start.4 = (bf16[4,64,768]{2,1,0:T(8,128)(2,1)S(1)}, bf16[4,64,768]{2,1,0:T(8,128)(2,1)S(1)}, u32[]{:S(2)}, u32[]{:S(2)}) collective-permute-start(bf16[4,64,768]{2,1,0:T(8,128)(2,1)S(1)} %pad_maximum_fusion.1.refs_0_), channel_id=1, source_target_pairs={{0,64},{64,128},{128,192},{192,0},{1,65},{65,129},{129,193},{193,1... | collective-permute-start | bytes 1179656 | tf_op jit(solution)/shard_map/ppermute | solution.py:193
  36.4 17.5 %collective-permute-start.10 = (bf16[4,64,768]{2,1,0:T(8,128)(2,1)S(1)}, bf16[4,64,768]{2,1,0:T(8,128)(2,1)S(1)}, u32[]{:S(2)}, u32[]{:S(2)}) collective-permute-start(bf16[4,64,768]{2,1,0:T(8,128)(2,1)S(1)} %pad_maximum_fusion.1.refs_0_), channel_id=1, source_target_pairs={{0,128},{64,192},{128,0},{192,64},{1,129},{65,193},{129,1},{193,65... | collective-permute-start | bytes 1179656 | tf_op jit(solution)/shard_map/ppermute | solution.py:193
  37.5 16.6 %collective-permute-start.8 = (bf16[4,64,768]{2,1,0:T(8,128)(2,1)S(1)}, bf16[4,64,768]{2,1,0:T(8,128)(2,1)S(1)}, u32[]{:S(2)}, u32[]{:S(2)}) collective-permute-start(bf16[4,64,768]{2,1,0:T(8,128)(2,1)S(1)} %pad_maximum_fusion.refs_0_), channel_id=1, source_target_pairs={{0,34},{2,0},{32,2},{34,32},{1,35},{3,1},{33,3},{35,33},{4,38},{6,... | collective-permute-start | bytes 1179656 | tf_op jit(solution)/shard_map/ppermute | solution.py:193
  39.6 14.5 %collective-permute-start.7 = (bf16[4,64,768]{2,1,0:T(8,128)(2,1)S(1)}, bf16[4,64,768]{2,1,0:T(8,128)(2,1)S(1)}, u32[]{:S(2)}, u32[]{:S(2)}) collective-permute-start(bf16[4,64,768]{2,1,0:T(8,128)(2,1)S(1)} %pad_maximum_fusion.refs_0_), channel_id=1, source_target_pairs={{0,2},{2,32},{32,34},{34,0},{1,3},{3,33},{33,35},{35,1},{4,6},{6,3... | collective-permute-start | bytes 1179656 | tf_op jit(solution)/shard_map/ppermute | solution.py:193
  51.0 9.3 %collective-permute-start.6 = (bf16[4,64,768]{2,1,0:T(8,128)(2,1)S(1)}, bf16[4,64,768]{2,1,0:T(8,128)(2,1)S(1)}, u32[]{:S(2)}, u32[]{:S(2)}) collective-permute-start(bf16[4,64,768]{2,1,0:T(8,128)(2,1)S(1)} %pad_maximum_fusion.refs_0_), channel_id=1, source_target_pairs={{0,32},{2,34},{32,0},{34,2},{1,33},{3,35},{33,1},{35,3},{4,36},{6,... | collective-permute-start | bytes 1179656 | tf_op jit(solution)/shard_map/ppermute | solution.py:193
  53.9 6.6 %copy-start.1 = (bf16[3584,512]{1,0:T(8,128)(2,1)S(1)}, bf16[3584,512]{1,0:T(8,128)(2,1)}, u32[]{:S(2)}) copy-start(bf16[3584,512]{1,0:T(8,128)(2,1)} %head.7) | copy-start | bytes 11010052
  54.0 7.7 %collective-permute-start.11 = (bf16[2,512,768]{2,1,0:T(8,128)(2,1)S(1)}, bf16[2,512,768]{2,1,0:T(8,128)(2,1)S(1)}, u32[]{:S(2)}, u32[]{:S(2)}) collective-permute-start(bf16[2,512,768]{2,1,0:T(8,128)(2,1)S(1)} %shard_map.68.rest.own), channel_id=1, source_target_pairs={{0,1},{1,0},{2,3},{3,2},{4,5},{5,4},{6,7},{7,6},{8,9},{9,8},{10,11... | collective-permute-start | bytes 4718600 | tf_op jit(solution)/shard_map/ppermute | solution.py:193
  60.4 1.7 %copy-start = (bf16[2304,512]{1,0:T(8,128)(2,1)S(1)}, bf16[2304,512]{1,0:T(8,128)(2,1)}, u32[]{:S(2)}) copy-start(bf16[2304,512]{1,0:T(8,128)(2,1)} %head.9) | copy-start | bytes 7077892
  60.4 3.5 %collective-permute-start.9 = (bf16[2,512,768]{2,1,0:T(8,128)(2,1)S(1)}, bf16[2,512,768]{2,1,0:T(8,128)(2,1)S(1)}, u32[]{:S(2)}, u32[]{:S(2)}) collective-permute-start(bf16[2,512,768]{2,1,0:T(8,128)(2,1)S(1)} %shard_map.67.own), channel_id=1, source_target_pairs={{0,1},{1,0},{2,3},{3,2},{4,5},{5,4},{6,7},{7,6},{8,9},{9,8},{10,11... | collective-permute-start | bytes 4718600 | tf_op jit(solution)/shard_map/ppermute | solution.py:193
  65.6 1.2 collective-permute-start.12
  94.3 3.0 %collective-permute-start.13 = (bf16[8,2,64,576]{3,2,1,0:T(8,128)(2,1)S(1)}, bf16[8,2,64,576]{3,2,1,0:T(8,128)(2,1)S(1)}, u32[]{:S(2)}, u32[]{:S(2)}) collective-permute-start(bf16[8,2,64,576]{3,2,1,0:T(8,128)(2,1)S(1)} %get-tuple-element.33), channel_id=1, source_target_pairs={{0,1},{1,0},{2,3},{3,2},{4,5},{5,4},{6,7},{7,6},{8,9},{9,8},{10,11... | collective-permute-start | bytes 3538952 | tf_op jit(solution)/shard_map/ppermute | solution.py:193
  120.6 11.8 %all-to-all-start.4 = ((bf16[8,8,576]{2,1,0:T(8,128)(2,1)}), bf16[8,8,576]{2,1,0:T(8,128)(2,1)S(1)}, u32[]{:S(2)}, u32[]{:S(2)}) async-start(bf16[8,8,576]{2,1,0:T(8,128)(2,1)} %bitcast.1), calls=%async_computation.4 | async-start | bytes 163840 | tf_op jit(solution)/shard_map/all_to_all | solution.py:279

commit v3 on v2

v3 whole, which is shorter than its diff:
```python
import functools
import jax
import jax.numpy as jnp
from jax import lax
from jax.experimental import pallas as pl
from jax.experimental.pallas import tpu as pltpu
from jax.sharding import Mesh, PartitionSpec as P

F32 = jnp.float32
BF16 = jnp.bfloat16
STEPS = (0, 2, 1, 3)
VMEM = pl.BlockSpec(memory_space=pltpu.VMEM)
HBM = pl.BlockSpec(memory_space=pltpu.HBM)
PARAMS = pltpu.CompilerParams(vmem_limit_bytes=16 * 1024 * 1024)


def place(parts, role, full):
    tokens = parts[0].shape[1]
    x = lax.axis_index("x")
    y = lax.axis_index("yh") * 2 + lax.axis_index("yl")
    for part, step in zip(parts, STEPS):
        for at, by in enumerate(STEPS):
            sx = jnp.where(role == 0, lax.rem(x - by + 4, 4), lax.rem(x - step + 4, 4))
            sy = jnp.where(role == 0, lax.rem(y - step + 4, 4), lax.rem(y - by + 4, 4))
            block = sx * 2 + lax.div(sy, 2)
            rows = pl.ds(pl.multiple_of(block * tokens, tokens), tokens)
            full[lax.rem(sy, 2), rows, :] = part[at]


def head_rows(low, core, head):
    width = head.shape[0] // 4
    return head[pl.ds(pl.multiple_of((low * 2 + core) * width, width), width), :]


def products(full, core, student, teacher, cols):
    wt, ws = teacher.shape[0] // 4, student.shape[0] // 4
    slog = tlog = None
    for low in range(2):
        cols[low] = full[low, :, wt : wt + ws]
        s = jnp.dot(cols[low], head_rows(low, core, student), preferred_element_type=F32)
        t = jnp.dot(
            full[low, :, :wt], head_rows(low, core, teacher), preferred_element_type=F32
        )
        slog, tlog = (s, t) if low == 0 else (slog + s, tlog + t)
    return slog, tlog


def stack_kernel(*refs):
    for at, part in enumerate(refs[:-1]):
        refs[-1][at] = part[...]


def fetch_kernel(student_at, teacher_at, student, teacher, sems):
    copies = [
        pltpu.make_async_copy(student_at, student, sems.at[0]),
        pltpu.make_async_copy(teacher_at, teacher, sems.at[1]),
    ]
    for copy in copies:
        copy.start()
    for copy in copies:
        copy.wait()


def own_kernel(*refs):
    parts, (student, teacher, slog, tlog, cols, full) = refs[:4], refs[4:]
    core = lax.axis_index("c")
    place(parts, core, full)
    slog[...], tlog[...] = products(full, core, student, teacher, cols)


def sibling_kernel(*refs):
    parts, (student, teacher, slog, tlog, et_ref, es_ref, stats, cols, full) = (
        refs[:4],
        refs[4:],
    )
    core = 1 - lax.axis_index("c")
    place(parts, core, full)
    sl, tl = products(full, core, student, teacher, cols)
    tl, sl = tl + tlog[...], sl + slog[...]
    tm = jnp.max(tl, axis=1, keepdims=True)
    sm = jnp.max(sl, axis=1, keepdims=True)
    et, es = jnp.exp(tl - tm), jnp.exp(sl - sm)
    et_ref[...] = et
    es_ref[...] = es
    stat_cols = (
        tm,
        sm,
        jnp.sum(et, axis=1, keepdims=True),
        jnp.sum(es, axis=1, keepdims=True),
        jnp.sum(et * (tl - sl), axis=1, keepdims=True),
    )
    lane = lax.broadcasted_iota(jnp.int32, (tl.shape[0], 128), 1)
    wide = jnp.zeros((tl.shape[0], 128), F32)
    for k, col in enumerate(stat_cols):
        wide = jnp.where(lane == k, col, wide)
    stats[...] = wide.T[:8]


def merge(gathered):
    n = gathered.shape[0]
    part = [gathered[p] for p in range(n)]
    tm, sm = part[0][0:1], part[0][1:2]
    for p in range(1, n):
        tm = jnp.maximum(tm, part[p][0:1])
        sm = jnp.maximum(sm, part[p][1:2])
    tt = st = cr = jnp.zeros_like(tm)
    for p in range(n):
        tscale = jnp.exp(part[p][0:1] - tm)
        tt = tt + part[p][2:3] * tscale
        st = st + part[p][3:4] * jnp.exp(part[p][1:2] - sm)
        cr = cr + part[p][4:5] * tscale
    return tm, sm, tt, st, cr


def merge_kernel(*refs):
    sources, out = refs[:-1], refs[-1]
    part = jnp.stack([r[...] for r in sources]) if len(sources) > 1 else sources[0]
    rows = merge(part)
    value = jnp.concatenate(list(rows) + [jnp.zeros_like(rows[0])] * 3, axis=0)
    for p in range(out.shape[0]):
        out[p] = value


def grad_kernel(gathered, own, et, es, head, kl, grad, theirs):
    tm, sm, tt, st, cr = merge(gathered)
    kl[...] = (cr / tt - tm - jnp.log(tt) + sm + jnp.log(st)).reshape(kl.shape)
    mine_stats = own[...]
    tscale = jnp.exp(mine_stats[0:1] - tm) / tt
    sscale = jnp.exp(mine_stats[1:2] - sm) / st
    row = lax.broadcasted_iota(jnp.int32, (128, tm.shape[1]), 0)
    wide = jnp.where(row == 0, tscale, jnp.where(row == 1, sscale, 0.0)).T
    grad[...] = (es[...] * wide[:, 1:2] - et[...] * wide[:, 0:1]).astype(BF16)
    rows_part(grad, head, 1 - lax.axis_index("c"), theirs)


def rows_part(grad, head, core, out):
    width = out.shape[3]
    for low in range(2):
        start = pl.multiple_of((low * 2 + core) * width, width)
        value = lax.dot_general(
            grad[...],
            head[pl.ds(start, width), :],
            (((1,), (1,)), ((), ())),
            preferred_element_type=F32,
        )
        out[:, low] = value.reshape(out.shape[0], out.shape[2], width).astype(out.dtype)


def mine_kernel(grad, head, mine):
    rows_part(grad, head, lax.axis_index("c"), mine)


def head_kernel(own, sibling, grad, out):
    c = lax.axis_index("c")
    width = own.shape[2]
    for low in range(2):
        for cols, core in ((own, c), (sibling, 1 - c)):
            start = pl.multiple_of((low * 2 + core) * width, width)
            out[pl.ds(start, width), :] = lax.dot_general(
                cols[low], grad[...], (((0,), (0,)), ((), ())), preferred_element_type=F32
            ).astype(BF16)


def split_kernel(mine, theirs, *outs):
    c, x = lax.axis_index("c"), lax.axis_index("x")
    y = lax.axis_index("yh") * 2 + lax.axis_index("yl")
    half, width = outs[0].shape[1], mine.shape[3]
    for k in range(4):
        for other in range(4):
            to_x = jnp.where(c == 0, lax.rem(x + k, 4), other)
            to_y = jnp.where(c == 0, other, lax.rem(y + k, 4))
            block, low = to_x * 2 + lax.div(to_y, 2), lax.rem(to_y, 2)
            value = mine[block, low] + theirs[block, low].astype(F32)
            value = value.astype(outs[k].dtype)
            outs[k][other, :, :width] = value[:half]
            outs[k][other, :, width:] = value[half:]


def step_kernel(*refs):
    parts, outs = refs[:4], refs[4:]
    y = lax.axis_index("yh") * 2 + lax.axis_index("yl")
    here = jnp.where(lax.axis_index("c") == 0, y, lax.axis_index("x"))
    for k in range(4):
        at = lax.rem(here + k, 4)
        value = parts[0][at]
        for part in parts[1:]:
            value = value + part[at].astype(F32)
        outs[k][...] = value.astype(outs[k].dtype)


def last_kernel(*refs):
    parts, out = refs[:4], refs[4]
    half, width = parts[0].shape[0], out.shape[1]
    value = parts[0][...]
    for part in parts[1:]:
        value = value + part[...].astype(F32)
    value = value.astype(BF16)
    out[:half] = value[:, :width]
    out[half:] = value[:, width:]


def call(kernel, operands, outs, scratch=(), flops=0, hbm_in=0):
    nbytes = sum(a.size * a.dtype.itemsize for a in list(operands) + list(outs))
    return pl.pallas_call(
        kernel,
        out_shape=outs,
        in_specs=[HBM] * hbm_in + [VMEM] * (len(operands) - hbm_in),
        out_specs=[VMEM] * len(outs),
        scratch_shapes=list(scratch),
        compiler_params=PARAMS,
        cost_estimate=pl.CostEstimate(flops=flops, bytes_accessed=nbytes, transcendentals=0),
    )(*operands)


def swap(value):
    return lax.ppermute(value, "c", [(0, 1), (1, 0)])


def both_ways(value, move, x_core):
    pairs = []
    for x in range(4):
        for y in range(4):
            for c in range(2):
                to = (move(x), y) if c == x_core else (x, move(y))
                pairs.append(((x * 4 + y) * 2 + c, (to[0] * 4 + to[1]) * 2 + c))
    return lax.ppermute(value, ("x", "yh", "yl", "c"), pairs)


def shift(value, k, x_core):
    return both_ways(value, lambda i: (i + k) % 4, x_core)


def shards(sizes, teacher_rows, student_rows, teacher_head, student_head):
    nz = sizes["z"]
    wt, ws = teacher_rows.shape[1], student_rows.shape[1]
    rows = teacher_rows.shape[0]
    tokens, total = nz * rows, 8 * nz * rows
    vocab = teacher_head.shape[1]
    fill = -(wt + ws) % 128

    both = jnp.concatenate(
        [teacher_rows, student_rows, jnp.zeros((rows, fill), BF16)], axis=1
    )
    part = lax.all_to_all(
        jnp.broadcast_to(both[None], (nz,) + both.shape), "z", 0, 0, tiled=True
    ).reshape(tokens, wt + ws + fill)
    (part,) = call(
        stack_kernel,
        [part] + [shift(part, k, 0) for k in STEPS[1:]],
        [jax.ShapeDtypeStruct((4, tokens, wt + ws + fill), BF16)],
    )
    part, student_late, teacher_late = lax.optimization_barrier(
        (part, student_head, teacher_head)
    )
    parts = [part] + [shift(part, k, 1) for k in STEPS[1:]]
    sds = jax.ShapeDtypeStruct
    logits, cols = sds((total, vocab), F32), sds((2, total, ws), BF16)
    scratch = [pltpu.VMEM((2, total, wt + ws + fill), BF16)]
    heads = call(
        fetch_kernel,
        [student_late, teacher_late],
        [sds(student_head.shape, BF16), sds(teacher_head.shape, BF16)],
        scratch=[pltpu.SemaphoreType.DMA((2,))],
        hbm_in=2,
    )
    first, heads = lax.optimization_barrier((parts[3], heads))
    there = [swap(p) for p in parts[:3] + [first]]
    slog, tlog, stud_own = call(
        own_kernel,
        parts + list(heads),
        [logits, logits, cols],
        scratch=scratch,
        flops=4 * total * (wt + ws) * vocab,
    )
    et, es, stats, stud_sib = call(
        sibling_kernel,
        there + list(heads) + [slog, tlog],
        [logits, logits, sds((8, total), F32), cols],
        scratch=scratch,
        flops=4 * total * (wt + ws) * vocab,
    )
    (gathered,) = call(
        merge_kernel, [stats, swap(stats)], [sds((16, 8, total), F32)]
    )
    gathered = lax.all_to_all(gathered, ("x", "yh", "yl"), 0, 0, tiled=True)
    (gathered,) = call(merge_kernel, [gathered], [sds((nz, 8, total), F32)])
    gathered = lax.all_to_all(gathered, "z", 0, 0, tiled=True)
    kl, grad, theirs = call(
        grad_kernel,
        [gathered, stats, et, es, student_head],
        [sds((total,), F32), sds((total, vocab), BF16), sds((8, 2, tokens, ws), BF16)],
        flops=4 * total * ws * vocab,
    )
    theirs = swap(theirs)
    (mine,) = call(
        mine_kernel,
        [grad, student_head],
        [sds((8, 2, tokens, ws), F32)],
        flops=4 * total * ws * vocab,
    )
    slots = [sds((4, tokens // 2, 2 * ws), F32 if k == 0 else BF16) for k in range(4)]
    parts = call(split_kernel, [mine, theirs], slots)
    parts = [parts[0]] + [shift(parts[k], k, 0) for k in (1, 2, 3)]
    slots = [sds((tokens // 2, 2 * ws), F32 if k == 0 else BF16) for k in range(4)]
    parts = call(step_kernel, parts, slots)
    parts = [parts[0]] + [shift(parts[k], k, 1) for k in (1, 2, 3)]
    (part,) = call(last_kernel, parts, [sds((tokens, ws), BF16)])
    part, grad = lax.optimization_barrier((part, grad))
    (head_grad,) = call(
        head_kernel,
        [stud_own, stud_sib, grad],
        [sds(student_head.shape, BF16)],
        flops=8 * total * ws * vocab,
    )
    part = lax.all_to_all(part.reshape(nz, rows, ws), "z", 0, 0, tiled=True)
    rows_grad = jnp.sum(part.astype(F32), axis=0).astype(BF16)
    return kl, rows_grad, head_grad


def program(mesh):
    vocab, tensor = ("x", "yh", "z"), ("yl", "c")
    placed = (
        P(vocab, tensor),
        P(vocab, tensor),
        P(None, vocab + tensor),
        P(None, vocab + tensor),
    )
    return jax.shard_map(
        functools.partial(shards, dict(mesh.shape)),
        mesh=mesh,
        in_specs=placed,
        out_specs=(P(), P(vocab, tensor), P(None, vocab + tensor)),
        check_vma=False,
    )


def solution(mesh):
    nz = mesh.shape["vocab"] // 8
    return program(
        Mesh(mesh.devices.reshape(4, 2, nz, 2, 2), ("x", "yh", "z", "yl", "c"))
    )
```

time: 134 us -> 128 us (0.955)
  blocking collectives: 66.3 us -> 46 us
  starting transfers between devices: 19.6 us -> 26.7 us
  local copies, waits for them, and re-layouts: 1.12 us -> 4.52 us
  waiting for transfers between devices: 32.6 us -> 36 us
    all_to_all x1 -> x0, blocking collectives: 22.2 us -> none  [shards(): part = lax.all_to_all(part, ('x', 'yh', 'yl'), 0, 0, tiled=True)]
    ppermute x14 -> x18, starting transfers between devices: 16.2 us -> 23.3 us  [the longest x12 18.7 us: both_ways(): return lax.ppermute(value, ('x', 'yh', 'yl', 'c'), pairs)]
    ppermute x14 -> x18, waiting for transfers between devices: 26.9 us -> 30.4 us  [the longest x12 26.7 us: both_ways(): return lax.ppermute(value, ('x', 'yh', 'yl', 'c'), pairs)]
    unnamed x4 -> x6, local copies, waits for them, and re-layouts: 0.29 us -> 3.71 us
    all_to_all x1, blocking collectives: 13.3 us -> 15.8 us  [shards(): gathered = lax.all_to_all(gathered, ('x', 'yh', 'yl'), 0, 0, tiled=True)]
  transfers between devices with their start and end apart: 15 -> 19, of which waited for: 10 -> 14; matrix products, arithmetic and copies ran while one was open for 0% -> 0% of each run, Pallas kernels for 5% -> 5%
where the time goes in v3:
time: 128 us; the launch traced here: 127 us
  blocking collectives  46 us (36%)
  waiting for transfers between devices  36 us (28%)
  starting transfers between devices  26.7 us (21%)
  Pallas kernels  12.4 us (10%)
  local copies, waits for them, and re-layouts  4.52 us (4%)
    ppermute x12, waiting for transfers between devices, both_ways(): return lax.ppermute(value, ('x', 'yh', 'yl', 'c'), pairs)  26.7 us
    all_to_all x1, blocking collectives, shards(): lax.all_to_all(jnp.broadcast_to(both[None], (nz,) + both.shape), 'z', 0,...  18.7 us
    ppermute x12, starting transfers between devices, both_ways(): return lax.ppermute(value, ('x', 'yh', 'yl', 'c'), pairs)  18.7 us
    all_to_all x1, blocking collectives, shards(): gathered = lax.all_to_all(gathered, ('x', 'yh', 'yl'), 0, 0, tiled=True)  15.8 us
    pallas_call x12, Pallas kernels, call(): pl.pallas_call(kernel, out_shape=outs, in_specs=[HBM] * hbm_in + [VMEM] *...  12.4 us
    all_to_all x1, blocking collectives, shards(): gathered = lax.all_to_all(gathered, 'z', 0, 0, tiled=True)  11.5 us
    all_to_all x1, waiting for transfers between devices, shards(): part = lax.all_to_all(part.reshape(nz, rows, ws), 'z', 0, 0, tiled=True)  5.64 us
    ppermute x6, starting transfers between devices, swap(): return lax.ppermute(value, 'c', [(0, 1), (1, 0)])  4.57 us
  transfers between devices with their start and end apart: 19, of which 14 were waited for; matrix products, arithmetic and copies ran while one was open for 0% of the time, Pallas kernels for 5%

profile of v3, /device:TPU:8, one launch (start us, length us, event | category | flops | bytes accessed | tf_op | source)
XLA Modules:
  0.0 127.0 jit_solution(11267857122650577207)
XLA Ops:
  0.6 0.8 concatenate.3
  1.5 18.7 %all_to_all.20 = bf16[8,8,1536]{2,1,0:T(8,128)(2,1)S(1)} all-to-all(bf16[8,8,1536]{2,1,0:T(8,128)(2,1)S(1)} %broadcast_in_dim.10), channel_id=1, replica_groups=mesh['x'=4,'yh'=2,'z'=8,'yl'=2,'c'=2] {'z'}, dimensions={0} | all-to-all | bytes 393216 | tf_op jit(solution)/shard_map/all_to_all | solution.py:244
  20.2 2.8 %collective-permute-start.2 = (bf16[64,1536]{1,0:T(8,128)(2,1)S(1)}, bf16[64,1536]{1,0:T(8,128)(2,1)S(1)}, u32[]{:S(2)}, u32[]{:S(2)}) collective-permute-start(bf16[64,1536]{1,0:T(8,128)(2,1)S(1)} %bitcast.2), channel_id=1, source_target_pairs={{0,192},{1,35},{2,194},{3,1},{32,224},{33,3},{34,226},{35,33},{64,... | collective-permute-start | bytes 589832 | tf_op jit(solution)/shard_map/ppermute | solution.py:226
  23.0 2.3 %collective-permute-start = (bf16[64,1536]{1,0:T(8,128)(2,1)S(1)}, bf16[64,1536]{1,0:T(8,128)(2,1)S(1)}, u32[]{:S(2)}, u32[]{:S(2)}) collective-permute-start(bf16[64,1536]{1,0:T(8,128)(2,1)S(1)} %bitcast.4), channel_id=1, source_target_pairs={{0,128},{1,33},{2,130},{3,35},{32,160},{33,1},{34,162},{35,3},{64,... | collective-permute-start | bytes 589832 | tf_op jit(solution)/shard_map/ppermute | solution.py:226
  25.2 0.9 collective-permute-done.2.refs_3_
  26.1 5.8 %collective-permute-done.1.refs_2_ = bf16[64,1536]{1,0:T(8,128)(2,1)S(1)} collective-permute-done((bf16[64,1536]{1,0:T(8,128)(2,1)S(1)}, bf16[64,1536]{1,0:T(8,128)(2,1)S(1)}, u32[]{:S(2)}, u32[]{:S(2)}) %collective-permute-start.1) | collective-permute-done | bytes 196640 | tf_op jit(solution)/shard_map/ppermute | solution.py:226
  31.9 0.1 shard_map.67.refs_0_
  32.0 0.5 collective-permute-start.8
  32.5 1.6 %collective-permute-start.6 = (bf16[4,64,1536]{2,1,0:T(8,128)(2,1)S(1)}, bf16[4,64,1536]{2,1,0:T(8,128)(2,1)S(1)}, u32[]{:S(2)}, u32[]{:S(2)}) collective-permute-start(bf16[4,64,1536]{2,1,0:T(8,128)(2,1)S(1)} %shard_map.67.refs_0_), channel_id=1, source_target_pairs={{0,2},{1,65},{2,32},{3,67},{32,34},{33,97},{34,0},{35,99},{64,66},... | collective-permute-start | bytes 2359304 | tf_op jit(solution)/shard_map/ppermute | solution.py:226
  34.1 3.5 %collective-permute-start.4 = (bf16[4,64,1536]{2,1,0:T(8,128)(2,1)S(1)}, bf16[4,64,1536]{2,1,0:T(8,128)(2,1)S(1)}, u32[]{:S(2)}, u32[]{:S(2)}) collective-permute-start(bf16[4,64,1536]{2,1,0:T(8,128)(2,1)S(1)} %shard_map.67.refs_0_), channel_id=1, source_target_pairs={{0,32},{1,129},{2,34},{3,131},{32,0},{33,161},{34,2},{35,163},{64,... | collective-permute-start | bytes 2359304 | tf_op jit(solution)/shard_map/ppermute | solution.py:226
  37.6 1.7 %copy-done = bf16[2304,512]{1,0:T(8,128)(2,1)S(1)} copy-done((bf16[2304,512]{1,0:T(8,128)(2,1)S(1)}, bf16[2304,512]{1,0:T(8,128)(2,1)}, u32[]{:S(2)}) %copy-start) | copy-done | bytes 2359320
  39.3 2.0 %copy-done.2 = bf16[3584,512]{1,0:T(8,128)(2,1)S(1)} copy-done((bf16[3584,512]{1,0:T(8,128)(2,1)S(1)}, bf16[3584,512]{1,0:T(8,128)(2,1)}, u32[]{:S(2)}) %copy-start.2) | copy-done | bytes 3670040
  41.3 0.4 shard_map.68
  41.7 2.3 %collective-permute-done.8.refs_3_ = bf16[4,64,1536]{2,1,0:T(8,128)(2,1)S(1)} collective-permute-done((bf16[4,64,1536]{2,1,0:T(8,128)(2,1)S(1)}, bf16[4,64,1536]{2,1,0:T(8,128)(2,1)S(1)}, u32[]{:S(2)}, u32[]{:S(2)}) %collective-permute-start.8) | collective-permute-done | bytes 786464 | tf_op jit(solution)/shard_map/ppermute | solution.py:226
  44.1 1.4 %collective-permute-done.6.refs_2_ = bf16[4,64,1536]{2,1,0:T(8,128)(2,1)S(1)} collective-permute-done((bf16[4,64,1536]{2,1,0:T(8,128)(2,1)S(1)}, bf16[4,64,1536]{2,1,0:T(8,128)(2,1)S(1)}, u32[]{:S(2)}, u32[]{:S(2)}) %collective-permute-start.6) | collective-permute-done | bytes 786464 | tf_op jit(solution)/shard_map/ppermute | solution.py:226
  45.5 3.9 %collective-permute-start.7 = (bf16[4,64,1536]{2,1,0:T(8,128)(2,1)S(1)}, bf16[4,64,1536]{2,1,0:T(8,128)(2,1)S(1)}, u32[]{:S(2)}, u32[]{:S(2)}) collective-permute-start(bf16[4,64,1536]{2,1,0:T(8,128)(2,1)S(1)} %collective-permute-done.6.refs_2_), channel_id=1, source_target_pairs={{0,1},{1,0},{2,3},{3,2},{4,5},{5,4},{6,7},{7,6},{8,9},{9,8},{10,11... | collective-permute-start | bytes 2359304 | tf_op jit(solution)/shard_map/ppermute | solution.py:216
  49.4 4.1 %collective-permute-done.4.refs_1_ = bf16[4,64,1536]{2,1,0:T(8,128)(2,1)S(1)} collective-permute-done((bf16[4,64,1536]{2,1,0:T(8,128)(2,1)S(1)}, bf16[4,64,1536]{2,1,0:T(8,128)(2,1)S(1)}, u32[]{:S(2)}, u32[]{:S(2)}) %collective-permute-start.4) | collective-permute-done | bytes 786464 | tf_op jit(solution)/shard_map/ppermute | solution.py:226
  53.5 0.5 collective-permute-start.9
  54.0 2.3 %shard_map.69 = (f32[512,512]{1,0:T(8,128)S(1)}, f32[512,512]{1,0:T(8,128)S(1)}, bf16[2,512,576]{2,1,0:T(8,128)(2,1)S(1)}) custom-call(bf16[4,64,1536]{2,1,0:T(8,128)(2,1)S(1)} %shard_map.67.refs_0_, bf16[4,64,1536]{2,1,0:T(8,128)(2,1)S(1)} %collective-permute-done.4.refs_1_, bf16[4,64,1536]{2,1,0:T(8,128)(2,1)S(1)} %collective-permute-done.6.refs_2_, ...), custom_call_target="tpu_custom_call" | custom-call | flops 1543503872 | bytes 12451840 | tf_op jit(solution)/shard_map/pallas_call | solution.py:204
  56.3 0.6 collective-permute-done.9.refs_3_
  56.9 2.7 %shard_map.70 = (f32[512,512]{1,0:T(8,128)S(1)}, f32[512,512]{1,0:T(8,128)S(1)}, f32[8,512]{1,0:T(8,128)S(1)}, bf16[2,512,576]{2,1,0:T(8,128)(2,1)S(1)}) custom-call(bf16[4,64,1536]{2,1,0:T(8,128)(2,1)S(1)} %collective-permute-done.3.refs_0_, bf16[4,64,1536]{2,1,0:T(8,128)(2,1)S(1)} %collective-permute-done.5.refs_1_, ...), custom_call_target="tpu_custom_call" | custom-call | flops 1543503872 | bytes 14565376 | tf_op jit(solution)/shard_map/pallas_call | solution.py:204
  59.6 0.2 collective-permute-start.10
  59.8 1.0 collective-permute-done.10.refs_1_
  60.9 15.8 %all_to_all.21.refs_0_ = f32[16,8,512]{2,1,0:T(8,128)S(1)} all-to-all(f32[16,8,512]{2,1,0:T(8,128)S(1)} %shard_map.71), channel_id=1, replica_groups=mesh['x'=4,'yh'=2,'z'=8,'yl'=2,'c'=2] {'x','yh','yl'}, dimensions={0} | all-to-all | bytes 524288 | tf_op jit(solution)/shard_map/all_to_all | solution.py:285
  76.7 0.1 shard_map.72
  76.8 11.5 %all_to_all.22.gathered = f32[8,8,512]{2,1,0:T(8,128)S(1)} all-to-all(f32[8,8,512]{2,1,0:T(8,128)S(1)} %shard_map.72), channel_id=1, replica_groups=mesh['x'=4,'yh'=2,'z'=8,'yl'=2,'c'=2] {'z'}, dimensions={0} | all-to-all | bytes 262144 | tf_op jit(solution)/shard_map/all_to_all | solution.py:287
  88.3 1.8 %shard_map.73 = (f32[512]{0:T(512)}, bf16[512,512]{1,0:T(8,128)(2,1)S(1)}, bf16[8,2,64,576]{3,2,1,0:T(8,128)(2,1)S(1)}) custom-call(f32[8,8,512]{2,1,0:T(8,128)S(1)} %all_to_all.22.gathered, f32[8,512]{1,0:T(8,128)S(1)} %get-tuple-element.41.refs_0_.own, f32[512,512]{1,0:T(8,128)S(1)} %get-tuple-element.42.et, f32[512,512]{1,0:T(8,128)S(1)} %get-tuple-element.43.es, ...), custom_call_target="tpu_custom_call" | custom-call | flops 603979776 | bytes 6309888 | tf_op jit(solution)/shard_map/pallas_call | solution.py:204
  90.1 0.0 collective-permute-start.11
  90.1 1.0 shard_map.74.mine
  91.1 2.0 %collective-permute-done.11.theirs = bf16[8,2,64,576]{3,2,1,0:T(8,128)(2,1)S(1)} collective-permute-done((bf16[8,2,64,576]{3,2,1,0:T(8,128)(2,1)S(1)}, bf16[8,2,64,576]{3,2,1,0:T(8,128)(2,1)S(1)}, u32[]{:S(2)}, u32[]{:S(2)}) %collective-permute-start.11) | collective-permute-done | bytes 1179680 | tf_op jit(solution)/shard_map/ppermute | solution.py:216
  93.2 0.3 shard_map.75
  93.5 0.1 collective-permute-start.12
  93.6 2.6 %collective-permute-start.13 = (bf16[4,32,1152]{2,1,0:T(8,128)(2,1)S(1)}, bf16[4,32,1152]{2,1,0:T(8,128)(2,1)S(1)}, u32[]{:S(2)}, u32[]{:S(2)}) collective-permute-start(bf16[4,32,1152]{2,1,0:T(8,128)(2,1)S(1)} %get-tuple-element.49), channel_id=1, source_target_pairs={{0,128},{1,33},{2,130},{3,35},{32,160},{33,1},{34,162},{35,3},{64,... | collective-permute-start | bytes 884744 | tf_op jit(solution)/shard_map/ppermute | solution.py:226
  96.2 1.3 %collective-permute-start.14 = (bf16[4,32,1152]{2,1,0:T(8,128)(2,1)S(1)}, bf16[4,32,1152]{2,1,0:T(8,128)(2,1)S(1)}, u32[]{:S(2)}, u32[]{:S(2)}) collective-permute-start(bf16[4,32,1152]{2,1,0:T(8,128)(2,1)S(1)} %get-tuple-element.50), channel_id=1, source_target_pairs={{0,192},{1,35},{2,194},{3,1},{32,224},{33,3},{34,226},{35,33},{64,... | collective-permute-start | bytes 884744 | tf_op jit(solution)/shard_map/ppermute | solution.py:226
  97.5 7.2 %collective-permute-done.12.refs_1_ = bf16[4,32,1152]{2,1,0:T(8,128)(2,1)S(1)} collective-permute-done((bf16[4,32,1152]{2,1,0:T(8,128)(2,1)S(1)}, bf16[4,32,1152]{2,1,0:T(8,128)(2,1)S(1)}, u32[]{:S(2)}, u32[]{:S(2)}) %collective-permute-start.12) | collective-permute-done | bytes 294944 | tf_op jit(solution)/shard_map/ppermute | solution.py:226
  104.7 0.9 collective-permute-done.14.refs_3_
  105.6 0.1 shard_map.76
  105.7 1.1 collective-permute-start.15
  106.8 2.7 %collective-permute-start.16 = (bf16[32,1152]{1,0:T(8,128)(2,1)S(1)}, bf16[32,1152]{1,0:T(8,128)(2,1)S(1)}, u32[]{:S(2)}, u32[]{:S(2)}) collective-permute-start(bf16[32,1152]{1,0:T(8,128)(2,1)S(1)} %get-tuple-element.53), channel_id=1, source_target_pairs={{0,32},{1,129},{2,34},{3,131},{32,0},{33,161},{34,2},{35,163},{64,... | collective-permute-start | bytes 221192 | tf_op jit(solution)/shard_map/ppermute | solution.py:226
  109.5 0.3 collective-permute-start.17
  109.8 0.3 collective-permute-done.15.refs_1_
  110.1 2.5 %collective-permute-done.16.refs_2_ = bf16[32,1152]{1,0:T(8,128)(2,1)S(1)} collective-permute-done((bf16[32,1152]{1,0:T(8,128)(2,1)S(1)}, bf16[32,1152]{1,0:T(8,128)(2,1)S(1)}, u32[]{:S(2)}, u32[]{:S(2)}) %collective-permute-start.16) | collective-permute-done | bytes 73760 | tf_op jit(solution)/shard_map/ppermute | solution.py:226
  112.7 1.2 collective-permute-done.17.refs_3_
  113.8 0.7 shard_map.77
  114.5 3.4 %all-to-all-start.3 = ((bf16[8,8,576]{2,1,0:T(8,128)(2,1)}), bf16[8,8,576]{2,1,0:T(8,128)(2,1)S(1)}, u32[]{:S(2)}, u32[]{:S(2)}) async-start(bf16[8,8,576]{2,1,0:T(8,128)(2,1)} %bitcast.1), calls=%async_computation.3 | async-start | bytes 163840 | tf_op jit(solution)/shard_map/all_to_all | solution.py:315
  117.9 2.8 %shard_map.78 = bf16[2304,512]{1,0:T(8,128)(2,1)} custom-call(bf16[2,512,576]{2,1,0:T(8,128)(2,1)S(1)} %get-tuple-element.56.own, bf16[2,512,576]{2,1,0:T(8,128)(2,1)S(1)} %get-tuple-element.57.sibling, bf16[512,512]{1,0:T(8,128)(2,1)S(1)} %get-tuple-element.58.grad), custom_call_target="tpu_custom_call" | custom-call | flops 1207959552 | bytes 5242880 | tf_op jit(solution)/shard_map/pallas_call | solution.py:204
  120.7 5.6 %all-to-all-done.3 = bf16[8,8,576]{2,1,0:T(8,128)(2,1)S(1)} async-done(((bf16[8,8,576]{2,1,0:T(8,128)(2,1)}), bf16[8,8,576]{2,1,0:T(8,128)(2,1)S(1)}, u32[]{:S(2)}, u32[]{:S(2)}) %all-to-all-start.3) | async-done | bytes 73760 | tf_op jit(solution)/shard_map/all_to_all | solution.py:315
  126.4 0.6 reduce_sum.12
  (15 shorter events, 0.1 us)
Async XLA Ops:
  20.2 5.9 %collective-permute-start.2 = (bf16[64,1536]{1,0:T(8,128)(2,1)S(1)}, bf16[64,1536]{1,0:T(8,128)(2,1)S(1)}, u32[]{:S(2)}, u32[]{:S(2)}) collective-permute-start(bf16[64,1536]{1,0:T(8,128)(2,1)S(1)} %bitcast.2), channel_id=1, source_target_pairs={{0,192},{1,35},{2,194},{3,1},{32,224},{33,3},{34,226},{35,33},{64,... | collective-permute-start | bytes 589832 | tf_op jit(solution)/shard_map/ppermute | solution.py:226
  23.0 9.0 %collective-permute-start.1 = (bf16[64,1536]{1,0:T(8,128)(2,1)S(1)}, bf16[64,1536]{1,0:T(8,128)(2,1)S(1)}, u32[]{:S(2)}, u32[]{:S(2)}) collective-permute-start(bf16[64,1536]{1,0:T(8,128)(2,1)S(1)} %bitcast.3), channel_id=1, source_target_pairs={{0,64},{1,3},{2,66},{3,33},{32,96},{33,35},{34,98},{35,1},{64,128}... | collective-permute-start | bytes 589832 | tf_op jit(solution)/shard_map/ppermute | solution.py:226
  23.0 9.0 %collective-permute-start = (bf16[64,1536]{1,0:T(8,128)(2,1)S(1)}, bf16[64,1536]{1,0:T(8,128)(2,1)S(1)}, u32[]{:S(2)}, u32[]{:S(2)}) collective-permute-start(bf16[64,1536]{1,0:T(8,128)(2,1)S(1)} %bitcast.4), channel_id=1, source_target_pairs={{0,128},{1,33},{2,130},{3,35},{32,160},{33,1},{34,162},{35,3},{64,... | collective-permute-start | bytes 589832 | tf_op jit(solution)/shard_map/ppermute | solution.py:226
  32.0 12.1 %collective-permute-start.8 = (bf16[4,64,1536]{2,1,0:T(8,128)(2,1)S(1)}, bf16[4,64,1536]{2,1,0:T(8,128)(2,1)S(1)}, u32[]{:S(2)}, u32[]{:S(2)}) collective-permute-start(bf16[4,64,1536]{2,1,0:T(8,128)(2,1)S(1)} %shard_map.67.refs_0_), channel_id=1, source_target_pairs={{0,34},{1,193},{2,0},{3,195},{32,2},{33,225},{34,32},{35,227},{64,... | collective-permute-start | bytes 2359304 | tf_op jit(solution)/shard_map/ppermute | solution.py:226
  32.5 13.0 %collective-permute-start.6 = (bf16[4,64,1536]{2,1,0:T(8,128)(2,1)S(1)}, bf16[4,64,1536]{2,1,0:T(8,128)(2,1)S(1)}, u32[]{:S(2)}, u32[]{:S(2)}) collective-permute-start(bf16[4,64,1536]{2,1,0:T(8,128)(2,1)S(1)} %shard_map.67.refs_0_), channel_id=1, source_target_pairs={{0,2},{1,65},{2,32},{3,67},{32,34},{33,97},{34,0},{35,99},{64,66},... | collective-permute-start | bytes 2359304 | tf_op jit(solution)/shard_map/ppermute | solution.py:226
  34.1 19.4 %collective-permute-start.4 = (bf16[4,64,1536]{2,1,0:T(8,128)(2,1)S(1)}, bf16[4,64,1536]{2,1,0:T(8,128)(2,1)S(1)}, u32[]{:S(2)}, u32[]{:S(2)}) collective-permute-start(bf16[4,64,1536]{2,1,0:T(8,128)(2,1)S(1)} %shard_map.67.refs_0_), channel_id=1, source_target_pairs={{0,32},{1,129},{2,34},{3,131},{32,0},{33,161},{34,2},{35,163},{64,... | collective-permute-start | bytes 2359304 | tf_op jit(solution)/shard_map/ppermute | solution.py:226
  37.6 18.7 %collective-permute-start.3 = (bf16[4,64,1536]{2,1,0:T(8,128)(2,1)S(1)}, bf16[4,64,1536]{2,1,0:T(8,128)(2,1)S(1)}, u32[]{:S(2)}, u32[]{:S(2)}) collective-permute-start(bf16[4,64,1536]{2,1,0:T(8,128)(2,1)S(1)} %shard_map.67.refs_0_), channel_id=1, source_target_pairs={{0,1},{1,0},{2,3},{3,2},{4,5},{5,4},{6,7},{7,6},{8,9},{9,8},{10,11... | collective-permute-start | bytes 2359304 | tf_op jit(solution)/shard_map/ppermute | solution.py:216
  37.6 1.7 %copy-start = (bf16[2304,512]{1,0:T(8,128)(2,1)S(1)}, bf16[2304,512]{1,0:T(8,128)(2,1)}, u32[]{:S(2)}) copy-start(bf16[2304,512]{1,0:T(8,128)(2,1)} %head.3) | copy-start | bytes 7077892
  39.3 2.0 %copy-start.2 = (bf16[3584,512]{1,0:T(8,128)(2,1)S(1)}, bf16[3584,512]{1,0:T(8,128)(2,1)}, u32[]{:S(2)}) copy-start(bf16[3584,512]{1,0:T(8,128)(2,1)} %teacher_at) | copy-start | bytes 11010052
  45.5 10.8 %collective-permute-start.7 = (bf16[4,64,1536]{2,1,0:T(8,128)(2,1)S(1)}, bf16[4,64,1536]{2,1,0:T(8,128)(2,1)S(1)}, u32[]{:S(2)}, u32[]{:S(2)}) collective-permute-start(bf16[4,64,1536]{2,1,0:T(8,128)(2,1)S(1)} %collective-permute-done.6.refs_2_), channel_id=1, source_target_pairs={{0,1},{1,0},{2,3},{3,2},{4,5},{5,4},{6,7},{7,6},{8,9},{9,8},{10,11... | collective-permute-start | bytes 2359304 | tf_op jit(solution)/shard_map/ppermute | solution.py:216
  53.5 2.8 %collective-permute-start.5 = (bf16[4,64,1536]{2,1,0:T(8,128)(2,1)S(1)}, bf16[4,64,1536]{2,1,0:T(8,128)(2,1)S(1)}, u32[]{:S(2)}, u32[]{:S(2)}) collective-permute-start(bf16[4,64,1536]{2,1,0:T(8,128)(2,1)S(1)} %collective-permute-done.4.refs_1_), channel_id=1, source_target_pairs={{0,1},{1,0},{2,3},{3,2},{4,5},{5,4},{6,7},{7,6},{8,9},{9,8},{10,11... | collective-permute-start | bytes 2359304 | tf_op jit(solution)/shard_map/ppermute | solution.py:216
  53.5 3.4 %collective-permute-start.9 = (bf16[4,64,1536]{2,1,0:T(8,128)(2,1)S(1)}, bf16[4,64,1536]{2,1,0:T(8,128)(2,1)S(1)}, u32[]{:S(2)}, u32[]{:S(2)}) collective-permute-start(bf16[4,64,1536]{2,1,0:T(8,128)(2,1)S(1)} %collective-permute-done.8.refs_3_), channel_id=1, source_target_pairs={{0,1},{1,0},{2,3},{3,2},{4,5},{5,4},{6,7},{7,6},{8,9},{9,8},{10,11... | collective-permute-start | bytes 2359304 | tf_op jit(solution)/shard_map/ppermute | solution.py:216
  56.9 31.4 %copy-start.1 = (bf16[2304,512]{1,0:T(8,128)(2,1)S(1)}, bf16[2304,512]{1,0:T(8,128)(2,1)}, u32[]{:S(2)}) copy-start(bf16[2304,512]{1,0:T(8,128)(2,1)} %head.3) | copy-start | bytes 7077892
  59.6 1.2 collective-permute-start.10
  90.1 3.0 %collective-permute-start.11 = (bf16[8,2,64,576]{3,2,1,0:T(8,128)(2,1)S(1)}, bf16[8,2,64,576]{3,2,1,0:T(8,128)(2,1)S(1)}, u32[]{:S(2)}, u32[]{:S(2)}) collective-permute-start(bf16[8,2,64,576]{3,2,1,0:T(8,128)(2,1)S(1)} %get-tuple-element.46), channel_id=1, source_target_pairs={{0,1},{1,0},{2,3},{3,2},{4,5},{5,4},{6,7},{7,6},{8,9},{9,8},{10,11... | collective-permute-start | bytes 3538952 | tf_op jit(solution)/shard_map/ppermute | solution.py:216
  93.5 11.2 %collective-permute-start.12 = (bf16[4,32,1152]{2,1,0:T(8,128)(2,1)S(1)}, bf16[4,32,1152]{2,1,0:T(8,128)(2,1)S(1)}, u32[]{:S(2)}, u32[]{:S(2)}) collective-permute-start(bf16[4,32,1152]{2,1,0:T(8,128)(2,1)S(1)} %get-tuple-element.48), channel_id=1, source_target_pairs={{0,64},{1,3},{2,66},{3,33},{32,96},{33,35},{34,98},{35,1},{64,128}... | collective-permute-start | bytes 884744 | tf_op jit(solution)/shard_map/ppermute | solution.py:226
  93.6 11.1 %collective-permute-start.13 = (bf16[4,32,1152]{2,1,0:T(8,128)(2,1)S(1)}, bf16[4,32,1152]{2,1,0:T(8,128)(2,1)S(1)}, u32[]{:S(2)}, u32[]{:S(2)}) collective-permute-start(bf16[4,32,1152]{2,1,0:T(8,128)(2,1)S(1)} %get-tuple-element.49), channel_id=1, source_target_pairs={{0,128},{1,33},{2,130},{3,35},{32,160},{33,1},{34,162},{35,3},{64,... | collective-permute-start | bytes 884744 | tf_op jit(solution)/shard_map/ppermute | solution.py:226
  96.2 9.4 %collective-permute-start.14 = (bf16[4,32,1152]{2,1,0:T(8,128)(2,1)S(1)}, bf16[4,32,1152]{2,1,0:T(8,128)(2,1)S(1)}, u32[]{:S(2)}, u32[]{:S(2)}) collective-permute-start(bf16[4,32,1152]{2,1,0:T(8,128)(2,1)S(1)} %get-tuple-element.50), channel_id=1, source_target_pairs={{0,192},{1,35},{2,194},{3,1},{32,224},{33,3},{34,226},{35,33},{64,... | collective-permute-start | bytes 884744 | tf_op jit(solution)/shard_map/ppermute | solution.py:226
  105.7 4.4 %collective-permute-start.15 = (bf16[32,1152]{1,0:T(8,128)(2,1)S(1)}, bf16[32,1152]{1,0:T(8,128)(2,1)S(1)}, u32[]{:S(2)}, u32[]{:S(2)}) collective-permute-start(bf16[32,1152]{1,0:T(8,128)(2,1)S(1)} %get-tuple-element.52), channel_id=1, source_target_pairs={{0,2},{1,65},{2,32},{3,67},{32,34},{33,97},{34,0},{35,99},{64,66},... | collective-permute-start | bytes 221192 | tf_op jit(solution)/shard_map/ppermute | solution.py:226
  106.8 5.9 %collective-permute-start.16 = (bf16[32,1152]{1,0:T(8,128)(2,1)S(1)}, bf16[32,1152]{1,0:T(8,128)(2,1)S(1)}, u32[]{:S(2)}, u32[]{:S(2)}) collective-permute-start(bf16[32,1152]{1,0:T(8,128)(2,1)S(1)} %get-tuple-element.53), channel_id=1, source_target_pairs={{0,32},{1,129},{2,34},{3,131},{32,0},{33,161},{34,2},{35,163},{64,... | collective-permute-start | bytes 221192 | tf_op jit(solution)/shard_map/ppermute | solution.py:226
  109.5 4.4 %collective-permute-start.17 = (bf16[32,1152]{1,0:T(8,128)(2,1)S(1)}, bf16[32,1152]{1,0:T(8,128)(2,1)S(1)}, u32[]{:S(2)}, u32[]{:S(2)}) collective-permute-start(bf16[32,1152]{1,0:T(8,128)(2,1)S(1)} %get-tuple-element.54), channel_id=1, source_target_pairs={{0,34},{1,193},{2,0},{3,195},{32,2},{33,225},{34,32},{35,227},{64,... | collective-permute-start | bytes 221192 | tf_op jit(solution)/shard_map/ppermute | solution.py:226
  114.5 11.8 %all-to-all-start.3 = ((bf16[8,8,576]{2,1,0:T(8,128)(2,1)}), bf16[8,8,576]{2,1,0:T(8,128)(2,1)S(1)}, u32[]{:S(2)}, u32[]{:S(2)}) async-start(bf16[8,8,576]{2,1,0:T(8,128)(2,1)} %bitcast.1), calls=%async_computation.3 | async-start | bytes 163840 | tf_op jit(solution)/shard_map/all_to_all | solution.py:315

commit v4 on v3

--- a/solution.py
+++ b/solution.py
@@ -301,17 +301,18 @@
     slots = [sds((4, tokens // 2, 2 * ws), F32 if k == 0 else BF16) for k in range(4)]
     parts = call(split_kernel, [mine, theirs], slots)
     parts = [parts[0]] + [shift(parts[k], k, 0) for k in (1, 2, 3)]
-    slots = [sds((tokens // 2, 2 * ws), F32 if k == 0 else BF16) for k in range(4)]
-    parts = call(step_kernel, parts, slots)
-    parts = [parts[0]] + [shift(parts[k], k, 1) for k in (1, 2, 3)]
-    (part,) = call(last_kernel, parts, [sds((tokens, ws), BF16)])
-    part, grad = lax.optimization_barrier((part, grad))
     (head_grad,) = call(
         head_kernel,
         [stud_own, stud_sib, grad],
         [sds(student_head.shape, BF16)],
         flops=8 * total * ws * vocab,
     )
+    last, head_grad = lax.optimization_barrier((parts[3], head_grad))
+    parts = parts[:3] + [last]
+    slots = [sds((tokens // 2, 2 * ws), F32 if k == 0 else BF16) for k in range(4)]
+    parts = call(step_kernel, parts, slots)
+    parts = [parts[0]] + [shift(parts[k], k, 1) for k in (1, 2, 3)]
+    (part,) = call(last_kernel, parts, [sds((tokens, ws), BF16)])
     part = lax.all_to_all(part.reshape(nz, rows, ws), "z", 0, 0, tiled=True)
     rows_grad = jnp.sum(part.astype(F32), axis=0).astype(BF16)
     return kl, rows_grad, head_grad

time: 128 us -> 126 us (0.984)
  blocking collectives: 46 us -> 56.9 us
  waiting for transfers between devices: 36 us -> 28.6 us
  starting transfers between devices: 26.7 us -> 22.4 us
    all_to_all x0 -> x1, blocking collectives: none -> 10.9 us  [shards(): part = lax.all_to_all(part.reshape(nz, rows, ws), 'z', 0, 0, tiled=True)]
    all_to_all x1 -> x0, waiting for transfers between devices: 5.64 us -> none  [shards(): part = lax.all_to_all(part.reshape(nz, rows, ws), 'z', 0, 0, tiled=True)]
    all_to_all x1 -> x0, starting transfers between devices: 3.36 us -> none  [shards(): part = lax.all_to_all(part.reshape(nz, rows, ws), 'z', 0, 0, tiled=True)]
    ppermute x12, waiting for transfers between devices: 26.7 us -> 24.9 us  [both_ways(): return lax.ppermute(value, ('x', 'yh', 'yl', 'c'), pairs)]
  transfers between devices with their start and end apart: 19 -> 18, of which waited for: 14 -> 13; matrix products, arithmetic and copies ran while one was open for 0% -> 0% of each run, Pallas kernels for 5% -> 5%
where the time goes in v4:
time: 126 us
  blocking collectives  56.9 us (45%)
  waiting for transfers between devices  28.6 us (23%)
  starting transfers between devices  22.4 us (18%)
  Pallas kernels  11.8 us (9%)
  local copies, waits for them, and re-layouts  4.52 us (4%)
    ppermute x12, waiting for transfers between devices, both_ways(): return lax.ppermute(value, ('x', 'yh', 'yl', 'c'), pairs)  24.9 us
    all_to_all x1, blocking collectives, shards(): lax.all_to_all(jnp.broadcast_to(both[None], (nz,) + both.shape), 'z', 0,...  18.7 us
    ppermute x12, starting transfers between devices, both_ways(): return lax.ppermute(value, ('x', 'yh', 'yl', 'c'), pairs)  17.9 us
    all_to_all x1, blocking collectives, shards(): gathered = lax.all_to_all(gathered, ('x', 'yh', 'yl'), 0, 0, tiled=True)  15.8 us
    pallas_call x12, Pallas kernels, call(): pl.pallas_call(kernel, out_shape=outs, in_specs=[HBM] * hbm_in + [VMEM] *...  11.8 us
    all_to_all x1, blocking collectives, shards(): gathered = lax.all_to_all(gathered, 'z', 0, 0, tiled=True)  11.5 us
    all_to_all x1, blocking collectives, shards(): part = lax.all_to_all(part.reshape(nz, rows, ws), 'z', 0, 0, tiled=True)  10.9 us
    ppermute x6, starting transfers between devices, swap(): return lax.ppermute(value, 'c', [(0, 1), (1, 0)])  4.57 us
  transfers between devices with their start and end apart: 18, of which 13 were waited for; matrix products, arithmetic and copies ran while one was open for 0% of the time, Pallas kernels for 5%

profile of v4, /device:TPU:8, one launch (start us, length us, event | category | flops | bytes accessed | tf_op | source)
XLA Modules:
  0.0 125.6 jit_solution(12345978942804517374)
XLA Ops:
  0.6 0.8 concatenate.3
  1.5 18.7 %all_to_all.20 = bf16[8,8,1536]{2,1,0:T(8,128)(2,1)S(1)} all-to-all(bf16[8,8,1536]{2,1,0:T(8,128)(2,1)S(1)} %broadcast_in_dim.10), channel_id=1, replica_groups=mesh['x'=4,'yh'=2,'z'=8,'yl'=2,'c'=2] {'z'}, dimensions={0} | all-to-all | bytes 393216 | tf_op jit(solution)/shard_map/all_to_all | solution.py:244
  20.2 2.8 %collective-permute-start.2 = (bf16[64,1536]{1,0:T(8,128)(2,1)S(1)}, bf16[64,1536]{1,0:T(8,128)(2,1)S(1)}, u32[]{:S(2)}, u32[]{:S(2)}) collective-permute-start(bf16[64,1536]{1,0:T(8,128)(2,1)S(1)} %bitcast.2), channel_id=1, source_target_pairs={{0,192},{1,35},{2,194},{3,1},{32,224},{33,3},{34,226},{35,33},{64,... | collective-permute-start | bytes 589832 | tf_op jit(solution)/shard_map/ppermute | solution.py:226
  23.0 0.0 collective-permute-start.1
  23.0 2.3 %collective-permute-start = (bf16[64,1536]{1,0:T(8,128)(2,1)S(1)}, bf16[64,1536]{1,0:T(8,128)(2,1)S(1)}, u32[]{:S(2)}, u32[]{:S(2)}) collective-permute-start(bf16[64,1536]{1,0:T(8,128)(2,1)S(1)} %bitcast.4), channel_id=1, source_target_pairs={{0,128},{1,33},{2,130},{3,35},{32,160},{33,1},{34,162},{35,3},{64,... | collective-permute-start | bytes 589832 | tf_op jit(solution)/shard_map/ppermute | solution.py:226
  25.2 0.9 collective-permute-done.2.refs_3_
  26.1 5.8 %collective-permute-done.1.refs_2_ = bf16[64,1536]{1,0:T(8,128)(2,1)S(1)} collective-permute-done((bf16[64,1536]{1,0:T(8,128)(2,1)S(1)}, bf16[64,1536]{1,0:T(8,128)(2,1)S(1)}, u32[]{:S(2)}, u32[]{:S(2)}) %collective-permute-start.1) | collective-permute-done | bytes 196640 | tf_op jit(solution)/shard_map/ppermute | solution.py:226
  31.9 0.1 shard_map.67.refs_0_
  32.0 0.5 collective-permute-start.8
  32.5 1.6 %collective-permute-start.6 = (bf16[4,64,1536]{2,1,0:T(8,128)(2,1)S(1)}, bf16[4,64,1536]{2,1,0:T(8,128)(2,1)S(1)}, u32[]{:S(2)}, u32[]{:S(2)}) collective-permute-start(bf16[4,64,1536]{2,1,0:T(8,128)(2,1)S(1)} %shard_map.67.refs_0_), channel_id=1, source_target_pairs={{0,2},{1,65},{2,32},{3,67},{32,34},{33,97},{34,0},{35,99},{64,66},... | collective-permute-start | bytes 2359304 | tf_op jit(solution)/shard_map/ppermute | solution.py:226
  34.1 3.5 %collective-permute-start.4 = (bf16[4,64,1536]{2,1,0:T(8,128)(2,1)S(1)}, bf16[4,64,1536]{2,1,0:T(8,128)(2,1)S(1)}, u32[]{:S(2)}, u32[]{:S(2)}) collective-permute-start(bf16[4,64,1536]{2,1,0:T(8,128)(2,1)S(1)} %shard_map.67.refs_0_), channel_id=1, source_target_pairs={{0,32},{1,129},{2,34},{3,131},{32,0},{33,161},{34,2},{35,163},{64,... | collective-permute-start | bytes 2359304 | tf_op jit(solution)/shard_map/ppermute | solution.py:226
  37.6 1.7 %copy-done = bf16[2304,512]{1,0:T(8,128)(2,1)S(1)} copy-done((bf16[2304,512]{1,0:T(8,128)(2,1)S(1)}, bf16[2304,512]{1,0:T(8,128)(2,1)}, u32[]{:S(2)}) %copy-start) | copy-done | bytes 2359320
  39.3 2.0 %copy-done.2 = bf16[3584,512]{1,0:T(8,128)(2,1)S(1)} copy-done((bf16[3584,512]{1,0:T(8,128)(2,1)S(1)}, bf16[3584,512]{1,0:T(8,128)(2,1)}, u32[]{:S(2)}) %copy-start.2) | copy-done | bytes 3670040
  41.3 0.4 shard_map.68
  41.7 2.3 %collective-permute-done.8.refs_3_ = bf16[4,64,1536]{2,1,0:T(8,128)(2,1)S(1)} collective-permute-done((bf16[4,64,1536]{2,1,0:T(8,128)(2,1)S(1)}, bf16[4,64,1536]{2,1,0:T(8,128)(2,1)S(1)}, u32[]{:S(2)}, u32[]{:S(2)}) %collective-permute-start.8) | collective-permute-done | bytes 786464 | tf_op jit(solution)/shard_map/ppermute | solution.py:226
  44.1 1.4 %collective-permute-done.6.refs_2_ = bf16[4,64,1536]{2,1,0:T(8,128)(2,1)S(1)} collective-permute-done((bf16[4,64,1536]{2,1,0:T(8,128)(2,1)S(1)}, bf16[4,64,1536]{2,1,0:T(8,128)(2,1)S(1)}, u32[]{:S(2)}, u32[]{:S(2)}) %collective-permute-start.6) | collective-permute-done | bytes 786464 | tf_op jit(solution)/shard_map/ppermute | solution.py:226
  45.5 3.9 %collective-permute-start.7 = (bf16[4,64,1536]{2,1,0:T(8,128)(2,1)S(1)}, bf16[4,64,1536]{2,1,0:T(8,128)(2,1)S(1)}, u32[]{:S(2)}, u32[]{:S(2)}) collective-permute-start(bf16[4,64,1536]{2,1,0:T(8,128)(2,1)S(1)} %collective-permute-done.6.refs_2_), channel_id=1, source_target_pairs={{0,1},{1,0},{2,3},{3,2},{4,5},{5,4},{6,7},{7,6},{8,9},{9,8},{10,11... | collective-permute-start | bytes 2359304 | tf_op jit(solution)/shard_map/ppermute | solution.py:216
  49.4 4.1 %collective-permute-done.4.refs_1_ = bf16[4,64,1536]{2,1,0:T(8,128)(2,1)S(1)} collective-permute-done((bf16[4,64,1536]{2,1,0:T(8,128)(2,1)S(1)}, bf16[4,64,1536]{2,1,0:T(8,128)(2,1)S(1)}, u32[]{:S(2)}, u32[]{:S(2)}) %collective-permute-start.4) | collective-permute-done | bytes 786464 | tf_op jit(solution)/shard_map/ppermute | solution.py:226
  53.5 0.5 collective-permute-start.9
  54.0 2.3 %shard_map.69 = (f32[512,512]{1,0:T(8,128)S(1)}, f32[512,512]{1,0:T(8,128)S(1)}, bf16[2,512,576]{2,1,0:T(8,128)(2,1)S(1)}) custom-call(bf16[4,64,1536]{2,1,0:T(8,128)(2,1)S(1)} %shard_map.67.refs_0_, bf16[4,64,1536]{2,1,0:T(8,128)(2,1)S(1)} %collective-permute-done.4.refs_1_, bf16[4,64,1536]{2,1,0:T(8,128)(2,1)S(1)} %collective-permute-done.6.refs_2_, ...), custom_call_target="tpu_custom_call" | custom-call | flops 1543503872 | bytes 12451840 | tf_op jit(solution)/shard_map/pallas_call | solution.py:204
  56.3 0.6 collective-permute-done.9.refs_3_
  56.9 2.7 %shard_map.70 = (f32[512,512]{1,0:T(8,128)S(1)}, f32[512,512]{1,0:T(8,128)S(1)}, f32[8,512]{1,0:T(8,128)S(1)}, bf16[2,512,576]{2,1,0:T(8,128)(2,1)S(1)}) custom-call(bf16[4,64,1536]{2,1,0:T(8,128)(2,1)S(1)} %collective-permute-done.3.refs_0_, bf16[4,64,1536]{2,1,0:T(8,128)(2,1)S(1)} %collective-permute-done.5.refs_1_, ...), custom_call_target="tpu_custom_call" | custom-call | flops 1543503872 | bytes 14565376 | tf_op jit(solution)/shard_map/pallas_call | solution.py:204
  59.6 0.2 collective-permute-start.10
  59.8 1.0 collective-permute-done.10.refs_1_
  60.9 15.8 %all_to_all.21.refs_0_ = f32[16,8,512]{2,1,0:T(8,128)S(1)} all-to-all(f32[16,8,512]{2,1,0:T(8,128)S(1)} %shard_map.71), channel_id=1, replica_groups=mesh['x'=4,'yh'=2,'z'=8,'yl'=2,'c'=2] {'x','yh','yl'}, dimensions={0} | all-to-all | bytes 524288 | tf_op jit(solution)/shard_map/all_to_all | solution.py:285
  76.7 0.1 shard_map.72
  76.8 11.5 %all_to_all.22.gathered = f32[8,8,512]{2,1,0:T(8,128)S(1)} all-to-all(f32[8,8,512]{2,1,0:T(8,128)S(1)} %shard_map.72), channel_id=1, replica_groups=mesh['x'=4,'yh'=2,'z'=8,'yl'=2,'c'=2] {'z'}, dimensions={0} | all-to-all | bytes 262144 | tf_op jit(solution)/shard_map/all_to_all | solution.py:287
  88.3 1.8 %shard_map.73 = (f32[512]{0:T(512)}, bf16[512,512]{1,0:T(8,128)(2,1)S(1)}, bf16[8,2,64,576]{3,2,1,0:T(8,128)(2,1)S(1)}) custom-call(f32[8,8,512]{2,1,0:T(8,128)S(1)} %all_to_all.22.gathered, f32[8,512]{1,0:T(8,128)S(1)} %get-tuple-element.41.refs_0_.own, f32[512,512]{1,0:T(8,128)S(1)} %get-tuple-element.42.et, f32[512,512]{1,0:T(8,128)S(1)} %get-tuple-element.43.es, ...), custom_call_target="tpu_custom_call" | custom-call | flops 603979776 | bytes 6309888 | tf_op jit(solution)/shard_map/pallas_call | solution.py:204
  90.1 0.0 collective-permute-start.11
  90.1 1.0 shard_map.74.mine
  91.1 2.0 %collective-permute-done.11.theirs = bf16[8,2,64,576]{3,2,1,0:T(8,128)(2,1)S(1)} collective-permute-done((bf16[8,2,64,576]{3,2,1,0:T(8,128)(2,1)S(1)}, bf16[8,2,64,576]{3,2,1,0:T(8,128)(2,1)S(1)}, u32[]{:S(2)}, u32[]{:S(2)}) %collective-permute-start.11) | collective-permute-done | bytes 1179680 | tf_op jit(solution)/shard_map/ppermute | solution.py:216
  93.2 0.3 shard_map.75
  93.5 1.3 collective-permute-start.14
  94.8 0.8 collective-permute-start.12
  95.6 1.3 %collective-permute-start.13 = (bf16[4,32,1152]{2,1,0:T(8,128)(2,1)S(1)}, bf16[4,32,1152]{2,1,0:T(8,128)(2,1)S(1)}, u32[]{:S(2)}, u32[]{:S(2)}) collective-permute-start(bf16[4,32,1152]{2,1,0:T(8,128)(2,1)S(1)} %get-tuple-element.49), channel_id=1, source_target_pairs={{0,128},{1,33},{2,130},{3,35},{32,160},{33,1},{34,162},{35,3},{64,... | collective-permute-start | bytes 884744 | tf_op jit(solution)/shard_map/ppermute | solution.py:226
  96.9 2.8 %shard_map.76 = bf16[2304,512]{1,0:T(8,128)(2,1)} custom-call(bf16[2,512,576]{2,1,0:T(8,128)(2,1)S(1)} %get-tuple-element.51.own, bf16[2,512,576]{2,1,0:T(8,128)(2,1)S(1)} %get-tuple-element.52.sibling, bf16[512,512]{1,0:T(8,128)(2,1)S(1)} %get-tuple-element.45.grad), custom_call_target="tpu_custom_call" | custom-call | flops 1207959552 | bytes 5242880 | tf_op jit(solution)/shard_map/pallas_call | solution.py:204
  99.7 0.6 collective-permute-done.14.refs_3_
  100.3 5.5 %collective-permute-done.12.refs_1_ = bf16[4,32,1152]{2,1,0:T(8,128)(2,1)S(1)} collective-permute-done((bf16[4,32,1152]{2,1,0:T(8,128)(2,1)S(1)}, bf16[4,32,1152]{2,1,0:T(8,128)(2,1)S(1)}, u32[]{:S(2)}, u32[]{:S(2)}) %collective-permute-start.12) | collective-permute-done | bytes 294944 | tf_op jit(solution)/shard_map/ppermute | solution.py:226
  105.9 0.1 shard_map.77
  106.0 0.9 collective-permute-start.15
  106.9 2.7 %collective-permute-start.16 = (bf16[32,1152]{1,0:T(8,128)(2,1)S(1)}, bf16[32,1152]{1,0:T(8,128)(2,1)S(1)}, u32[]{:S(2)}, u32[]{:S(2)}) collective-permute-start(bf16[32,1152]{1,0:T(8,128)(2,1)S(1)} %get-tuple-element.56), channel_id=1, source_target_pairs={{0,32},{1,129},{2,34},{3,131},{32,0},{33,161},{34,2},{35,163},{64,... | collective-permute-start | bytes 221192 | tf_op jit(solution)/shard_map/ppermute | solution.py:226
  109.6 0.2 collective-permute-start.17
  109.8 0.6 collective-permute-done.15.refs_1_
  110.4 2.3 %collective-permute-done.16.refs_2_ = bf16[32,1152]{1,0:T(8,128)(2,1)S(1)} collective-permute-done((bf16[32,1152]{1,0:T(8,128)(2,1)S(1)}, bf16[32,1152]{1,0:T(8,128)(2,1)S(1)}, u32[]{:S(2)}, u32[]{:S(2)}) %collective-permute-start.16) | collective-permute-done | bytes 73760 | tf_op jit(solution)/shard_map/ppermute | solution.py:226
  112.7 1.2 collective-permute-done.17.refs_3_
  114.0 0.1 shard_map.78
  114.1 10.9 %all_to_all.23 = bf16[8,8,576]{2,1,0:T(8,128)(2,1)S(1)} all-to-all(bf16[8,8,576]{2,1,0:T(8,128)(2,1)S(1)} %bitcast.6), channel_id=1, replica_groups=mesh['x'=4,'yh'=2,'z'=8,'yl'=2,'c'=2] {'z'}, dimensions={0} | all-to-all | bytes 147456 | tf_op jit(solution)/shard_map/all_to_all | solution.py:316
  125.0 0.6 reduce_sum.12
  (14 shorter events, 0.1 us)
Async XLA Ops:
  20.2 5.9 %collective-permute-start.2 = (bf16[64,1536]{1,0:T(8,128)(2,1)S(1)}, bf16[64,1536]{1,0:T(8,128)(2,1)S(1)}, u32[]{:S(2)}, u32[]{:S(2)}) collective-permute-start(bf16[64,1536]{1,0:T(8,128)(2,1)S(1)} %bitcast.2), channel_id=1, source_target_pairs={{0,192},{1,35},{2,194},{3,1},{32,224},{33,3},{34,226},{35,33},{64,... | collective-permute-start | bytes 589832 | tf_op jit(solution)/shard_map/ppermute | solution.py:226
  23.0 9.0 %collective-permute-start.1 = (bf16[64,1536]{1,0:T(8,128)(2,1)S(1)}, bf16[64,1536]{1,0:T(8,128)(2,1)S(1)}, u32[]{:S(2)}, u32[]{:S(2)}) collective-permute-start(bf16[64,1536]{1,0:T(8,128)(2,1)S(1)} %bitcast.3), channel_id=1, source_target_pairs={{0,64},{1,3},{2,66},{3,33},{32,96},{33,35},{34,98},{35,1},{64,128}... | collective-permute-start | bytes 589832 | tf_op jit(solution)/shard_map/ppermute | solution.py:226
  23.0 9.0 %collective-permute-start = (bf16[64,1536]{1,0:T(8,128)(2,1)S(1)}, bf16[64,1536]{1,0:T(8,128)(2,1)S(1)}, u32[]{:S(2)}, u32[]{:S(2)}) collective-permute-start(bf16[64,1536]{1,0:T(8,128)(2,1)S(1)} %bitcast.4), channel_id=1, source_target_pairs={{0,128},{1,33},{2,130},{3,35},{32,160},{33,1},{34,162},{35,3},{64,... | collective-permute-start | bytes 589832 | tf_op jit(solution)/shard_map/ppermute | solution.py:226
  32.0 12.1 %collective-permute-start.8 = (bf16[4,64,1536]{2,1,0:T(8,128)(2,1)S(1)}, bf16[4,64,1536]{2,1,0:T(8,128)(2,1)S(1)}, u32[]{:S(2)}, u32[]{:S(2)}) collective-permute-start(bf16[4,64,1536]{2,1,0:T(8,128)(2,1)S(1)} %shard_map.67.refs_0_), channel_id=1, source_target_pairs={{0,34},{1,193},{2,0},{3,195},{32,2},{33,225},{34,32},{35,227},{64,... | collective-permute-start | bytes 2359304 | tf_op jit(solution)/shard_map/ppermute | solution.py:226
  32.5 13.0 %collective-permute-start.6 = (bf16[4,64,1536]{2,1,0:T(8,128)(2,1)S(1)}, bf16[4,64,1536]{2,1,0:T(8,128)(2,1)S(1)}, u32[]{:S(2)}, u32[]{:S(2)}) collective-permute-start(bf16[4,64,1536]{2,1,0:T(8,128)(2,1)S(1)} %shard_map.67.refs_0_), channel_id=1, source_target_pairs={{0,2},{1,65},{2,32},{3,67},{32,34},{33,97},{34,0},{35,99},{64,66},... | collective-permute-start | bytes 2359304 | tf_op jit(solution)/shard_map/ppermute | solution.py:226
  34.1 19.4 %collective-permute-start.4 = (bf16[4,64,1536]{2,1,0:T(8,128)(2,1)S(1)}, bf16[4,64,1536]{2,1,0:T(8,128)(2,1)S(1)}, u32[]{:S(2)}, u32[]{:S(2)}) collective-permute-start(bf16[4,64,1536]{2,1,0:T(8,128)(2,1)S(1)} %shard_map.67.refs_0_), channel_id=1, source_target_pairs={{0,32},{1,129},{2,34},{3,131},{32,0},{33,161},{34,2},{35,163},{64,... | collective-permute-start | bytes 2359304 | tf_op jit(solution)/shard_map/ppermute | solution.py:226
  37.6 18.7 %collective-permute-start.3 = (bf16[4,64,1536]{2,1,0:T(8,128)(2,1)S(1)}, bf16[4,64,1536]{2,1,0:T(8,128)(2,1)S(1)}, u32[]{:S(2)}, u32[]{:S(2)}) collective-permute-start(bf16[4,64,1536]{2,1,0:T(8,128)(2,1)S(1)} %shard_map.67.refs_0_), channel_id=1, source_target_pairs={{0,1},{1,0},{2,3},{3,2},{4,5},{5,4},{6,7},{7,6},{8,9},{9,8},{10,11... | collective-permute-start | bytes 2359304 | tf_op jit(solution)/shard_map/ppermute | solution.py:216
  37.6 1.7 %copy-start = (bf16[2304,512]{1,0:T(8,128)(2,1)S(1)}, bf16[2304,512]{1,0:T(8,128)(2,1)}, u32[]{:S(2)}) copy-start(bf16[2304,512]{1,0:T(8,128)(2,1)} %head.3) | copy-start | bytes 7077892
  39.3 2.0 %copy-start.2 = (bf16[3584,512]{1,0:T(8,128)(2,1)S(1)}, bf16[3584,512]{1,0:T(8,128)(2,1)}, u32[]{:S(2)}) copy-start(bf16[3584,512]{1,0:T(8,128)(2,1)} %teacher_at) | copy-start | bytes 11010052
  45.5 10.8 %collective-permute-start.7 = (bf16[4,64,1536]{2,1,0:T(8,128)(2,1)S(1)}, bf16[4,64,1536]{2,1,0:T(8,128)(2,1)S(1)}, u32[]{:S(2)}, u32[]{:S(2)}) collective-permute-start(bf16[4,64,1536]{2,1,0:T(8,128)(2,1)S(1)} %collective-permute-done.6.refs_2_), channel_id=1, source_target_pairs={{0,1},{1,0},{2,3},{3,2},{4,5},{5,4},{6,7},{7,6},{8,9},{9,8},{10,11... | collective-permute-start | bytes 2359304 | tf_op jit(solution)/shard_map/ppermute | solution.py:216
  53.5 2.8 %collective-permute-start.5 = (bf16[4,64,1536]{2,1,0:T(8,128)(2,1)S(1)}, bf16[4,64,1536]{2,1,0:T(8,128)(2,1)S(1)}, u32[]{:S(2)}, u32[]{:S(2)}) collective-permute-start(bf16[4,64,1536]{2,1,0:T(8,128)(2,1)S(1)} %collective-permute-done.4.refs_1_), channel_id=1, source_target_pairs={{0,1},{1,0},{2,3},{3,2},{4,5},{5,4},{6,7},{7,6},{8,9},{9,8},{10,11... | collective-permute-start | bytes 2359304 | tf_op jit(solution)/shard_map/ppermute | solution.py:216
  53.5 3.4 %collective-permute-start.9 = (bf16[4,64,1536]{2,1,0:T(8,128)(2,1)S(1)}, bf16[4,64,1536]{2,1,0:T(8,128)(2,1)S(1)}, u32[]{:S(2)}, u32[]{:S(2)}) collective-permute-start(bf16[4,64,1536]{2,1,0:T(8,128)(2,1)S(1)} %collective-permute-done.8.refs_3_), channel_id=1, source_target_pairs={{0,1},{1,0},{2,3},{3,2},{4,5},{5,4},{6,7},{7,6},{8,9},{9,8},{10,11... | collective-permute-start | bytes 2359304 | tf_op jit(solution)/shard_map/ppermute | solution.py:216
  56.9 31.4 %copy-start.1 = (bf16[2304,512]{1,0:T(8,128)(2,1)S(1)}, bf16[2304,512]{1,0:T(8,128)(2,1)}, u32[]{:S(2)}) copy-start(bf16[2304,512]{1,0:T(8,128)(2,1)} %head.3) | copy-start | bytes 7077892
  59.6 1.2 collective-permute-start.10
  90.1 3.0 %collective-permute-start.11 = (bf16[8,2,64,576]{3,2,1,0:T(8,128)(2,1)S(1)}, bf16[8,2,64,576]{3,2,1,0:T(8,128)(2,1)S(1)}, u32[]{:S(2)}, u32[]{:S(2)}) collective-permute-start(bf16[8,2,64,576]{3,2,1,0:T(8,128)(2,1)S(1)} %get-tuple-element.46), channel_id=1, source_target_pairs={{0,1},{1,0},{2,3},{3,2},{4,5},{5,4},{6,7},{7,6},{8,9},{9,8},{10,11... | collective-permute-start | bytes 3538952 | tf_op jit(solution)/shard_map/ppermute | solution.py:216
  93.5 6.8 %collective-permute-start.14 = (bf16[4,32,1152]{2,1,0:T(8,128)(2,1)S(1)}, bf16[4,32,1152]{2,1,0:T(8,128)(2,1)S(1)}, u32[]{:S(2)}, u32[]{:S(2)}) collective-permute-start(bf16[4,32,1152]{2,1,0:T(8,128)(2,1)S(1)} %get-tuple-element.50), channel_id=1, source_target_pairs={{0,192},{1,35},{2,194},{3,1},{32,224},{33,3},{34,226},{35,33},{64,... | collective-permute-start | bytes 884744 | tf_op jit(solution)/shard_map/ppermute | solution.py:226
  94.8 11.1 %collective-permute-start.12 = (bf16[4,32,1152]{2,1,0:T(8,128)(2,1)S(1)}, bf16[4,32,1152]{2,1,0:T(8,128)(2,1)S(1)}, u32[]{:S(2)}, u32[]{:S(2)}) collective-permute-start(bf16[4,32,1152]{2,1,0:T(8,128)(2,1)S(1)} %get-tuple-element.48), channel_id=1, source_target_pairs={{0,64},{1,3},{2,66},{3,33},{32,96},{33,35},{34,98},{35,1},{64,128}... | collective-permute-start | bytes 884744 | tf_op jit(solution)/shard_map/ppermute | solution.py:226
  95.6 10.2 %collective-permute-start.13 = (bf16[4,32,1152]{2,1,0:T(8,128)(2,1)S(1)}, bf16[4,32,1152]{2,1,0:T(8,128)(2,1)S(1)}, u32[]{:S(2)}, u32[]{:S(2)}) collective-permute-start(bf16[4,32,1152]{2,1,0:T(8,128)(2,1)S(1)} %get-tuple-element.49), channel_id=1, source_target_pairs={{0,128},{1,33},{2,130},{3,35},{32,160},{33,1},{34,162},{35,3},{64,... | collective-permute-start | bytes 884744 | tf_op jit(solution)/shard_map/ppermute | solution.py:226
  106.0 4.4 %collective-permute-start.15 = (bf16[32,1152]{1,0:T(8,128)(2,1)S(1)}, bf16[32,1152]{1,0:T(8,128)(2,1)S(1)}, u32[]{:S(2)}, u32[]{:S(2)}) collective-permute-start(bf16[32,1152]{1,0:T(8,128)(2,1)S(1)} %get-tuple-element.55), channel_id=1, source_target_pairs={{0,2},{1,65},{2,32},{3,67},{32,34},{33,97},{34,0},{35,99},{64,66},... | collective-permute-start | bytes 221192 | tf_op jit(solution)/shard_map/ppermute | solution.py:226
  106.9 5.9 %collective-permute-start.16 = (bf16[32,1152]{1,0:T(8,128)(2,1)S(1)}, bf16[32,1152]{1,0:T(8,128)(2,1)S(1)}, u32[]{:S(2)}, u32[]{:S(2)}) collective-permute-start(bf16[32,1152]{1,0:T(8,128)(2,1)S(1)} %get-tuple-element.56), channel_id=1, source_target_pairs={{0,32},{1,129},{2,34},{3,131},{32,0},{33,161},{34,2},{35,163},{64,... | collective-permute-start | bytes 221192 | tf_op jit(solution)/shard_map/ppermute | solution.py:226
  109.6 4.4 %collective-permute-start.17 = (bf16[32,1152]{1,0:T(8,128)(2,1)S(1)}, bf16[32,1152]{1,0:T(8,128)(2,1)S(1)}, u32[]{:S(2)}, u32[]{:S(2)}) collective-permute-start(bf16[32,1152]{1,0:T(8,128)(2,1)S(1)} %get-tuple-element.57), channel_id=1, source_target_pairs={{0,34},{1,193},{2,0},{3,195},{32,2},{33,225},{34,32},{35,227},{64,... | collective-permute-start | bytes 221192 | tf_op jit(solution)/shard_map/ppermute | solution.py:226
